TPU v7x, 32 devices: a whole 2x2x4 slice. The times are simulated.
32 devices in a mesh: seq: 8 (over z, x), tp: 4 (over y, core).
Axes of the slice: x: 2, y: 2, z: 4, core: 2. Of those that a mesh axis runs over, the one named last changes fastest.
Arguments:
- inputs: bfloat16 [6144, 2048], P(('seq', 'tp')), may hold values from -6 to 6
- out_grad: bfloat16 [6144, 2048], P(('seq', 'tp')), may hold values from -6 to 6
- seq_lengths: int32 [2], replicated, may hold values from 1025 to 4864, as said below
- log_decay: float32 [6144, 16], P('seq', 'tp'), may hold values from -1 to 0, as said below
- mixer_weight: float32 [4, 2048, 2048], P(None, 'seq', 'tp'), may hold values from -0.125 to 0.125
- output_weight: float32 [2048, 2048], P('tp', 'seq'), may hold values from -0.125 to 0.125
- glu_weight: float32 [2, 2048, 5632], P(None, 'seq', 'tp'), may hold values from -0.125 to 0.125
- down_weight: float32 [5632, 2048], P('tp', 'seq'), may hold values from -0.078125 to 0.078125
- mixer_first: float32 [4, 2048, 2048], P(None, 'seq', 'tp'), may hold values from -40 to 40
- output_first: float32 [2048, 2048], P('tp', 'seq'), may hold values from -40 to 40
- glu_first: float32 [2, 2048, 5632], P(None, 'seq', 'tp'), may hold values from -40 to 40
- down_first: float32 [5632, 2048], P('tp', 'seq'), may hold values from -40 to 40
- mixer_second: float32 [4, 2048, 2048], P(None, 'seq', 'tp'), may hold values from 92.16 to 1228.8
- output_second: float32 [2048, 2048], P('tp', 'seq'), may hold values from 92.16 to 1228.8
- glu_second: float32 [2, 2048, 5632], P(None, 'seq', 'tp'), may hold values from 92.16 to 1228.8
- down_second: float32 [5632, 2048], P('tp', 'seq'), may hold values from 92.16 to 1228.8
Outputs:
- block_out: bfloat16 [6144, 2048], P(('seq', 'tp'))
- input_grad: float32 [6144, 2048], P(('seq', 'tp'))
- mixer_new: float32 [4, 2048, 2048], P(None, 'seq', 'tp')
- output_new: float32 [2048, 2048], P('tp', 'seq')
- glu_new: float32 [2, 2048, 5632], P(None, 'seq', 'tp')
- down_new: float32 [5632, 2048], P('tp', 'seq')
- mixer_first_new: float32 [4, 2048, 2048], P(None, 'seq', 'tp')
- output_first_new: float32 [2048, 2048], P('tp', 'seq')
- glu_first_new: float32 [2, 2048, 5632], P(None, 'seq', 'tp')
- down_first_new: float32 [5632, 2048], P('tp', 'seq')
- mixer_second_new: float32 [4, 2048, 2048], P(None, 'seq', 'tp')
- output_second_new: float32 [2048, 2048], P('tp', 'seq')
- glu_second_new: float32 [2, 2048, 5632], P(None, 'seq', 'tp')
- down_second_new: float32 [5632, 2048], P('tp', 'seq')
Inputs may be any that keep to these rules, and one draw needn't show every extreme that they name: `seq_lengths`: sequence i fills ceil(count / 256) consecutive blocks, sequences in order from block 0 and together filling all 24 blocks; each fills 5 to 19 blocks, and one is exactly 4864 rows long. `log_decay`: every entry is negative.
All inputs are finite; a program needn't handle non-finite values.
Results may differ from a plain program's by a relative error of at most 0.014.
Values may be sent and summed in bfloat16 or wider, within the bound.
No kernel may reach another device: no remote copies, remote signals or barrier semaphores. Data moves between devices by JAX's collectives and lax.ppermute only.
A program may use at most 320 MiB of HBM per device.

v0:
```python
import jax
import jax.numpy as jnp
from jax import lax
from jax.sharding import PartitionSpec as P

D = 2048
HD = 128
BLK = 256
STEP = 10


NORM_EPS = 1e-06
BETA_ONE = 0.9
BETA_TWO = 0.95
ADAM_EPS = 1e-08
WEIGHT_DECAY = 0.1
LEARN_RATE = 0.02


def entering_2(value, axis, join, neutral):
    count, mine = (lax.axis_size(axis), lax.axis_index(axis))
    pieces = jax.tree.map(lambda part: lax.all_gather(part, axis), value)
    so_far = jax.tree.map(
        lambda part, zero: jnp.full_like(part, 0) + jnp.asarray(zero, part.dtype), value, neutral
    )

    def entering_lap(position, so_far):
        longer = join(so_far, jax.tree.map(lambda part: part[position], pieces))
        return jax.tree.map(lambda new, old: jnp.where(position < mine, new, old), longer, so_far)

    return lax.fori_loop(0, count - 1, entering_lap, so_far)


def carried_in(array, axis, combine, identity):
    count, place = (lax.axis_size(axis), lax.axis_index(axis))
    everything = jax.tree.map(
        lambda part, kind: lax.all_gather(part.astype(kind), axis),
        array,
        (jnp.bfloat16, jnp.bfloat16),
    )
    start = jax.tree.map(
        lambda part, zero: jnp.broadcast_to(jnp.asarray(zero, part.dtype), part.shape),
        array,
        identity,
    )

    def carried_lap(k, before):
        at = count - 1 - k
        reached = at > place
        new = combine(
            before, jax.tree.map(lambda part, own: part[at].astype(own.dtype), everything, array)
        )
        return jax.tree.map(lambda a, b: jnp.where(reached, a, b), new, before)

    return lax.fori_loop(0, count, carried_lap, start)


def layout(seq_lengths, first_block, block_count):
    blocks = (seq_lengths + BLK - 1) // BLK
    starts = jnp.cumsum(blocks) - blocks
    block_index = first_block + jnp.arange(block_count, dtype=jnp.int32)
    begins = starts[None, :] == block_index[:, None]
    keep_flags = 1.0 - jnp.any(begins, axis=1).astype(jnp.float32)
    owner_index = jnp.sum((starts[None, :] <= block_index[:, None]).astype(jnp.int32), axis=1) - 1
    chosen = jnp.arange(seq_lengths.shape[0], dtype=jnp.int32)[None, :] == owner_index[:, None]
    own_start = jnp.sum(jnp.where(chosen, starts[None, :], 0), axis=1)
    own_length = jnp.sum(jnp.where(chosen, seq_lengths[None, :], 0), axis=1)
    position = (block_index - own_start)[:, None] * BLK + jnp.arange(BLK, dtype=jnp.int32)[None, :]
    token_mask = position < own_length[:, None]
    return (keep_flags, token_mask.reshape(block_count * BLK))


def normalize(values):
    norm_scale = lax.rsqrt(jnp.mean(values * values, axis=-1, keepdims=True) + NORM_EPS)
    return (values * norm_scale, norm_scale)


def norm_back(normed, norm_scale, incoming):
    return norm_scale * (incoming - normed * jnp.mean(incoming * normed, axis=-1, keepdims=True))


def silu_slope(values):
    sigmoid_v = jax.nn.sigmoid(values)
    return sigmoid_v * (1.0 + values * (1.0 - sigmoid_v))


def chain_pair(earlier, later):
    return (earlier[0] * later[0], later[0][:, None, None] * earlier[1] + later[1])


def build_decays(cumulative):
    per_head = jnp.transpose(cumulative, (0, 2, 1))
    rows_in = per_head.shape[2]
    causal = jnp.arange(rows_in)[:, None] >= jnp.arange(rows_in)[None, :]
    log_gaps = jnp.minimum(per_head[:, :, :, None] - per_head[:, :, None, :], 0.0)
    return jnp.where(causal, jnp.exp(log_gaps), 0.0)


def fold_step(carried, pieces):
    factor, state_term = pieces
    return ((factor * carried[0], factor[:, None, None] * carried[1] + state_term), None)


def walk_forward(carried, pieces):
    factor, state_term, keep_flag = pieces
    return (factor[:, None, None] * carried + state_term, keep_flag * carried)


def unfold_step(carried, pieces):
    factor, state_term = pieces
    return (factor[:, None, None] * carried + state_term, None)


def walk_back(carried, pieces):
    factor, state_term = pieces
    return (factor[:, None, None] * carried + state_term, carried)


def sum_feed(glu_grad, down_grad):
    return (
        lax.psum_scatter(glu_grad, "seq", scatter_dimension=1, tiled=True),
        lax.psum_scatter(down_grad, "seq", scatter_dimension=1, tiled=True),
    )


def adamw_step(weight, first, second, gradient):
    first_new = BETA_ONE * first + (1.0 - BETA_ONE) * gradient
    second_new = BETA_TWO * second + (1.0 - BETA_TWO) * gradient * gradient
    fix_one = 1.0 - BETA_ONE**STEP
    fix_two = 1.0 - BETA_TWO**STEP
    update = first_new / fix_one / (jnp.sqrt(second_new / fix_two) + ADAM_EPS)
    return (weight - LEARN_RATE * (update + WEIGHT_DECAY * weight), first_new, second_new)


def local(
    inputs,
    out_grad,
    seq_lengths,
    log_decay,
    mixer_weight,
    output_weight,
    glu_weight,
    down_weight,
    mixer_first,
    output_first,
    glu_first,
    down_first,
    mixer_second,
    output_second,
    glu_second,
    down_second,
):
    group_rows = log_decay.shape[0]
    heads_here = log_decay.shape[1]
    blocks_here = group_rows // BLK
    width_here = heads_here * HD
    bf16 = jnp.bfloat16
    f32 = jnp.float32
    seq_place = lax.axis_index("seq")
    keep_flags, token_mask = layout(seq_lengths, seq_place * blocks_here, blocks_here)
    mask_col = token_mask[:, None]
    mask_float = mask_col.astype(f32)
    inputs_f = inputs.astype(f32)
    normed_one, scale_one = normalize(inputs_f)
    rows_one = lax.all_gather(normed_one.astype(bf16), "tp", axis=0, tiled=True)
    mixer_full, output_full, glu_full, down_full = (
        lax.all_gather(mixer_weight.astype(bf16), "seq", axis=1, tiled=True),
        lax.all_gather(output_weight.astype(bf16), "seq", axis=1, tiled=True),
        lax.all_gather(glu_weight.astype(bf16), "seq", axis=1, tiled=True),
        lax.all_gather(down_weight.astype(bf16), "seq", axis=1, tiled=True),
    )
    projected = jnp.einsum("td,jdc->jtc", rows_one, mixer_full, preferred_element_type=f32)
    query_pre = projected[0]
    key_pre = projected[1]
    value_pre = projected[2]
    gate_u = projected[3]
    zero_low = jnp.zeros((), bf16)
    queries = jax.nn.silu(query_pre).astype(bf16)
    keys_all = jnp.where(mask_col, jax.nn.silu(key_pre).astype(bf16), zero_low)
    values_all = jnp.where(mask_col, value_pre.astype(bf16), zero_low)
    block_shape = (blocks_here, BLK, heads_here, HD)
    query_blocks = queries.reshape(block_shape)
    key_blocks = keys_all.reshape(block_shape)
    value_blocks = values_all.reshape(block_shape)
    cumulative = jnp.cumsum(log_decay.reshape(blocks_here, BLK, heads_here), axis=1)
    block_ends = cumulative[:, -1, :]
    exp_cum = jnp.exp(cumulative)[..., None]
    exp_tail = jnp.exp(block_ends[:, None, :] - cumulative)[..., None]
    decays = build_decays(cumulative)
    scores = jnp.einsum("bthe,bshe->bhts", query_blocks, key_blocks, preferred_element_type=f32)
    block_probs = (scores * decays).astype(bf16)
    inner_part = jnp.einsum(
        "bhts,bshf->bthf", block_probs, value_blocks, preferred_element_type=f32
    )
    scaled_q = (query_blocks * exp_cum).astype(bf16)
    scaled_k = (key_blocks * exp_tail).astype(bf16)
    state_terms = jnp.einsum("bshe,bshf->bhef", scaled_k, value_blocks, preferred_element_type=f32)
    factors = keep_flags[:, None] * jnp.exp(block_ends)
    unit_factor = jnp.ones((heads_here,), f32)
    zero_state = jnp.zeros((heads_here, HD, HD), f32)
    (device_factor, device_state), _ = lax.scan(
        fold_step, (unit_factor, zero_state), (factors, state_terms)
    )
    entering_factor, entering = entering_2(
        (device_factor, device_state), "seq", chain_pair, (unit_factor, zero_state)
    )
    _, used_states = lax.scan(walk_forward, entering, (factors, state_terms, keep_flags))
    used_low = used_states.astype(bf16)
    outer_part = jnp.einsum("bthe,bhef->bthf", scaled_q, used_low, preferred_element_type=f32)
    mixer_out = (inner_part + outer_part).reshape(group_rows, width_here)
    squares = lax.psum(jnp.sum(mixer_out * mixer_out, axis=1), "tp")
    mixer_scale = lax.rsqrt(squares / D + NORM_EPS)[:, None]
    mixer_normed = mixer_out * mixer_scale
    joined = (mixer_normed * gate_u).astype(bf16)
    branch = lax.psum_scatter(
        jnp.dot(joined, output_full, preferred_element_type=f32),
        "tp",
        scatter_dimension=0,
        tiled=True,
    )
    middle = inputs_f + branch
    normed_two, scale_two = normalize(middle)
    rows_two, grad_rows = (
        lax.all_gather(normed_two.astype(bf16), "tp", axis=0, tiled=True),
        lax.all_gather(out_grad, "tp", axis=0, tiled=True),
    )
    glu_gates = jnp.einsum("td,jdc->jtc", rows_two, glu_full, preferred_element_type=f32)
    gate_left = glu_gates[0]
    gate_right = glu_gates[1]
    product = (gate_left * gate_right).astype(bf16)
    feed_out = lax.psum_scatter(
        jnp.dot(product, down_full, preferred_element_type=f32),
        "tp",
        scatter_dimension=0,
        tiled=True,
    )
    block_out = (middle + feed_out).astype(bf16)
    product_grad = jnp.einsum("td,cd->tc", grad_rows, down_full, preferred_element_type=f32)
    down_grad = jnp.einsum("tc,td->cd", product, grad_rows, preferred_element_type=f32)
    gate_grads = jnp.stack(
        [(product_grad * gate_right).astype(bf16), (product_grad * gate_left).astype(bf16)]
    )
    glu_grad = jnp.einsum("td,jtc->jdc", rows_two, gate_grads, preferred_element_type=f32)
    two_grad = lax.psum_scatter(
        jnp.einsum("jtc,jdc->td", gate_grads, glu_full, preferred_element_type=f32),
        "tp",
        scatter_dimension=0,
        tiled=True,
    )
    middle_grad = out_grad.astype(f32) + norm_back(normed_two, scale_two, two_grad)
    branch_grad = lax.all_gather(middle_grad.astype(bf16), "tp", axis=0, tiled=True)
    joined_grad = jnp.einsum("td,cd->tc", branch_grad, output_full, preferred_element_type=f32)
    output_grad = jnp.einsum("tc,td->cd", joined, branch_grad, preferred_element_type=f32)
    gate_grad = (joined_grad * mixer_normed).astype(bf16)
    normed_grad = joined_grad * gate_u
    row_dots = lax.psum(jnp.sum(normed_grad * mixer_normed, axis=1), "tp")
    mixed_grad = (mixer_scale * (normed_grad - mixer_normed * (row_dots / D)[:, None])).astype(bf16)
    grad_blocks = mixed_grad.reshape(block_shape)
    kept_terms = keep_flags[:, None, None, None] * jnp.einsum(
        "bthe,bthf->bhef", scaled_q, grad_blocks, preferred_element_type=f32
    )
    local_back, _ = lax.scan(unfold_step, zero_state, (factors, kept_terms), reverse=True)
    leaving_factor, leaving = carried_in(
        (device_factor, local_back), "seq", chain_pair, (unit_factor, zero_state)
    )
    _, state_grads = lax.scan(walk_back, leaving, (factors, kept_terms), reverse=True)
    state_low = state_grads.astype(bf16)
    scores_again = jnp.einsum(
        "bthe,bshe->bhts", query_blocks, key_blocks, preferred_element_type=f32
    )
    probs_again = (scores_again * decays).astype(bf16)
    value_dots = jnp.einsum(
        "bthf,bshf->bhts", grad_blocks, value_blocks, preferred_element_type=f32
    )
    score_grad = (value_dots * decays).astype(bf16)
    query_grad = (
        jnp.einsum("bhts,bshe->bthe", score_grad, key_blocks, preferred_element_type=f32)
        + jnp.einsum("bthf,bhef->bthe", grad_blocks, used_low, preferred_element_type=f32) * exp_cum
    )
    key_grad = (
        jnp.einsum("bhts,bthe->bshe", score_grad, query_blocks, preferred_element_type=f32)
        + jnp.einsum("bshf,bhef->bshe", value_blocks, state_low, preferred_element_type=f32)
        * exp_tail
    )
    value_grad = jnp.einsum(
        "bhts,bthf->bshf", probs_again, grad_blocks, preferred_element_type=f32
    ) + jnp.einsum("bshe,bhef->bshf", scaled_k, state_low, preferred_element_type=f32)
    proj_grads = jnp.stack(
        [
            (query_grad.reshape(group_rows, width_here) * silu_slope(query_pre)).astype(bf16),
            (key_grad.reshape(group_rows, width_here) * mask_float * silu_slope(key_pre)).astype(
                bf16
            ),
            (value_grad.reshape(group_rows, width_here) * mask_float).astype(bf16),
            gate_grad,
        ]
    )
    mixer_grad = jnp.einsum("td,jtc->jdc", rows_one, proj_grads, preferred_element_type=f32)
    one_grad = lax.psum_scatter(
        jnp.einsum("jtc,jdc->td", proj_grads, mixer_full, preferred_element_type=f32),
        "tp",
        scatter_dimension=0,
        tiled=True,
    )
    input_grad = middle_grad + norm_back(normed_one, scale_one, one_grad)
    mixer_sum, output_sum = (
        lax.psum_scatter(mixer_grad, "seq", scatter_dimension=1, tiled=True),
        lax.psum_scatter(output_grad, "seq", scatter_dimension=1, tiled=True),
    )
    glu_sum, down_sum = sum_feed(glu_grad, down_grad)
    mixer_new, mixer_first_new, mixer_second_new = adamw_step(
        mixer_weight, mixer_first, mixer_second, mixer_sum
    )
    output_new, output_first_new, output_second_new = adamw_step(
        output_weight, output_first, output_second, output_sum
    )
    glu_new, glu_first_new, glu_second_new = adamw_step(glu_weight, glu_first, glu_second, glu_sum)
    down_new, down_first_new, down_second_new = adamw_step(
        down_weight, down_first, down_second, down_sum
    )
    return (
        block_out,
        input_grad,
        mixer_new,
        output_new,
        glu_new,
        down_new,
        mixer_first_new,
        output_first_new,
        glu_first_new,
        down_first_new,
        mixer_second_new,
        output_second_new,
        glu_second_new,
        down_second_new,
    )


def solution(mesh):
    in_specs = (
        P(("seq", "tp"), None),
        P(("seq", "tp"), None),
        P(),
        P("seq", "tp"),
        P(None, "seq", "tp"),
        P("tp", "seq"),
        P(None, "seq", "tp"),
        P("tp", "seq"),
        P(None, "seq", "tp"),
        P("tp", "seq"),
        P(None, "seq", "tp"),
        P("tp", "seq"),
        P(None, "seq", "tp"),
        P("tp", "seq"),
        P(None, "seq", "tp"),
        P("tp", "seq"),
    )
    out_specs = (
        P(("seq", "tp"), None),
        P(("seq", "tp"), None),
        P(None, "seq", "tp"),
        P("tp", "seq"),
        P(None, "seq", "tp"),
        P("tp", "seq"),
        P(None, "seq", "tp"),
        P("tp", "seq"),
        P(None, "seq", "tp"),
        P("tp", "seq"),
        P(None, "seq", "tp"),
        P("tp", "seq"),
        P(None, "seq", "tp"),
        P("tp", "seq"),
    )
    return jax.shard_map(local, mesh=mesh, in_specs=in_specs, out_specs=out_specs, check_vma=False)
```

profile of v0, /device:TPU:0, one launch (start us, length us, event | category | flops | bytes accessed | tf_op | source)
XLA Modules:
  0.0 1949.2 jit_solution(13113935569620702870)
XLA Ops:
  19.8 22.4 %all-gather.15.cloned.1.call-done = bf16[768,2048]{1,0:T(8,128)(2,1)} async-done(((bf16[192,2048]{1,0:T(8,128)(2,1)}), bf16[768,2048]{1,0:T(8,128)(2,1)}) %all-gather.15.cloned.1.call-update) | async-done | bytes 3145744 | tf_op jit(solution)/shard_map/all_gather | solution.py:165
  42.2 128.0 %all-gather.17.cloned.1.call-done = bf16[4,2048,512]{1,2,0:T(8,128)(2,1)} async-done(((bf16[4,256,512]{1,2,0:T(8,128)(2,1)}), bf16[4,2048,512]{1,2,0:T(8,128)(2,1)}) %all-gather.17.cloned.1.call-update) | async-done | bytes 8388624 | tf_op jit(solution)/shard_map/all_gather | solution.py:167
  204.3 18.8 all-reduce
  223.2 17.3 all-gather.31.cloned.1.call-done
  263.9 28.7 %all-gather.19.cloned.1.call-done = bf16[512,2048]{1,0:T(8,128)(2,1)} async-done(((bf16[512,256]{1,0:T(8,128)(2,1)}), bf16[512,2048]{1,0:T(8,128)(2,1)}) %all-gather.19.cloned.1.call-update) | async-done | bytes 2097168 | tf_op jit(solution)/shard_map/all_gather | solution.py:168
  302.0 53.5 %reduce-scatter.9.cloned.1.call-done = f32[192,2048]{1,0:T(8,128)} async-done(((f32[768,2048]{1,0:T(8,128)}), f32[192,2048]{1,0:T(8,128)}) %reduce-scatter.9.cloned.1.call-update) | async-done | bytes 1572880 | tf_op jit(solution)/shard_map/reduce_scatter | solution.py:215
  361.6 160.4 %all-gather.23.cloned.1.call-done = bf16[2,2048,1408]{2,1,0:T(8,128)(2,1)} async-done(((bf16[2,256,1408]{2,1,0:T(8,128)(2,1)}), bf16[2,2048,1408]{2,1,0:T(8,128)(2,1)}) %all-gather.23.cloned.1.call-update) | async-done | bytes 11534352 | tf_op jit(solution)/shard_map/all_gather | solution.py:169
  522.0 29.0 %all-gather.21.cloned.1.call-done = bf16[768,2048]{1,0:T(8,128)(2,1)} async-done(((bf16[192,2048]{1,0:T(8,128)(2,1)}), bf16[768,2048]{1,0:T(8,128)(2,1)}) %all-gather.21.cloned.1.call-update) | async-done | bytes 3145744 | tf_op jit(solution)/shard_map/all_gather | solution.py:224
  550.9 15.6 convolution_bitcast_fusion.2
  566.6 14.6 all-gather.27.cloned.1.call-done
  581.1 96.4 %all-gather.25.cloned.1.call-done = bf16[1408,2048]{1,0:T(8,128)(2,1)} async-done(((bf16[1408,256]{1,0:T(8,128)(2,1)}), bf16[1408,2048]{1,0:T(8,128)(2,1)}) %all-gather.25.cloned.1.call-update) | async-done | bytes 5767184 | tf_op jit(solution)/shard_map/all_gather | solution.py:170
  691.0 13.7 convolution_bitcast_fusion.3
  705.2 56.2 %reduce-scatter.13.cloned.1.call-done = f32[192,2048]{1,0:T(8,128)} async-done(((f32[768,2048]{1,0:T(8,128)}), f32[192,2048]{1,0:T(8,128)}) %reduce-scatter.13.cloned.1.call-update) | async-done | bytes 1572880 | tf_op jit(solution)/shard_map/reduce_scatter | solution.py:244
  764.9 28.6 %all-gather.29.cloned.1.call-done = bf16[768,2048]{1,0:T(8,128)(2,1)} async-done(((bf16[192,2048]{1,0:T(8,128)(2,1)}), bf16[768,2048]{1,0:T(8,128)(2,1)}) %all-gather.29.cloned.1.call-update) | async-done | bytes 3145744 | tf_op jit(solution)/shard_map/all_gather | solution.py:251
  813.5 11.5 fusion.58
  825.9 21.7 %all-reduce.1 = bf16[32]{0:T(256)(128)(2,1)S(1)} all-reduce(bf16[32]{0:T(256)(128)(2,1)S(1)} %dynamic-update-slice.1), channel_id=4, replica_groups=mesh['seq'=8,'tp'=4] {'seq'}, use_global_device_ids=true, to_apply=%add.1 | all-reduce | flops 32 | bytes 128
  925.9 16.5 convolution_bitcast_fusion
  942.5 12.8 convolution_bitcast_fusion.1
  971.4 79.0 %reduce-scatter.23.cloned.1.call-done = f32[1408,256]{1,0:T(8,128)} async-done(((f32[1408,2048]{1,0:T(8,128)}), f32[1408,256]{1,0:T(8,128)}) %reduce-scatter.23.cloned.1.call-update) | async-done | bytes 1441808 | tf_op jit(solution)/shard_map/reduce_scatter | solution.py:122
  1055.7 85.7 %reduce-scatter.19.cloned.1.call-done = f32[512,256]{1,0:T(8,128)} async-done(((f32[512,2048]{1,0:T(8,128)}), f32[512,256]{1,0:T(8,128)}) %reduce-scatter.19.cloned.1.call-update) | async-done | bytes 524304 | tf_op jit(solution)/shard_map/reduce_scatter | solution.py:308
  1144.0 58.1 %reduce-scatter.15.cloned.1.call-done = f32[192,2048]{1,0:T(8,128)} async-done(((f32[768,2048]{1,0:T(8,128)}), f32[192,2048]{1,0:T(8,128)}) %reduce-scatter.15.cloned.1.call-update) | async-done | bytes 1572880 | tf_op jit(solution)/shard_map/reduce_scatter | solution.py:299
  1203.9 59.0 %reduce-scatter.11.cloned.1.call-done = f32[192,2048]{1,0:T(8,128)} async-done(((f32[768,2048]{1,0:T(8,128)}), f32[192,2048]{1,0:T(8,128)}) %reduce-scatter.11.cloned.1.call-update) | async-done | bytes 1572880 | tf_op jit(solution)/shard_map/reduce_scatter | solution.py:231
  1267.6 373.9 %reduce-scatter.21.cloned.1.call-done = f32[2,256,1408]{1,2,0:T(8,128)} async-done(((f32[2,2048,1408]{1,2,0:T(8,128)}), f32[2,256,1408]{1,2,0:T(8,128)}) %reduce-scatter.21.cloned.1.call-update) | async-done | bytes 2883600 | tf_op jit(solution)/shard_map/reduce_scatter | solution.py:121
  1659.8 267.8 %reduce-scatter.17.cloned.1.call-done = f32[4,256,512]{1,2,0:T(8,128)} async-done(((f32[4,2048,512]{1,2,0:T(8,128)}), f32[4,256,512]{1,2,0:T(8,128)}) %reduce-scatter.17.cloned.1.call-update) | async-done | bytes 2097168 | tf_op jit(solution)/shard_map/reduce_scatter | solution.py:307
  (308 shorter events, 286.7 us)
Async XLA Ops:
  7.2 35.1 %all-gather.15.cloned.1.call-start = ((), (), s32[]{:S(2)}) async-start(), calls=%async_computation.8 | async-start | bytes 3932160 | tf_op jit(solution)/shard_map/all_gather | solution.py:165
  10.9 159.4 %all-gather.17.cloned.1.call-start = ((), (), s32[]{:S(2)}) async-start(), calls=%async_computation.9 | async-start | bytes 9437184 | tf_op jit(solution)/shard_map/all_gather | solution.py:167
  14.5 226.0 %all-gather.31.cloned.1.call-start = ((), (), s32[]{:S(2)}) async-start(), calls=%async_computation.24 | async-start | bytes 2359296 | tf_op jit(solution)/shard_map/all_gather | solution.py:22
  192.8 99.8 %all-gather.19.cloned.1.call-start = ((), (), s32[]{:S(2)}) async-start(), calls=%async_computation.10 | async-start | bytes 2359296 | tf_op jit(solution)/shard_map/all_gather | solution.py:168
  193.7 161.8 %reduce-scatter.9.cloned.1.call-start = ((), (), s32[]{:S(2)}) async-start(), calls=%async_computation.11 | async-start | bytes 7864320 | tf_op jit(solution)/shard_map/reduce_scatter | solution.py:215
  298.7 223.2 %all-gather.23.cloned.1.call-start = ((), (), s32[]{:S(2)}) async-start(), calls=%async_computation.13 | async-start | bytes 12976128 | tf_op jit(solution)/shard_map/all_gather | solution.py:169
  301.9 249.0 %all-gather.21.cloned.1.call-start = ((), (), s32[]{:S(2)}) async-start(), calls=%async_computation.12 | async-start | bytes 3932160 | tf_op jit(solution)/shard_map/all_gather | solution.py:224
  358.4 222.7 %all-gather.27.cloned.1.call-start = ((), (), s32[]{:S(2)}) async-start(), calls=%async_computation.16 | async-start | bytes 3932160 | tf_op jit(solution)/shard_map/all_gather | solution.py:225
  359.2 318.4 %all-gather.25.cloned.1.call-start = ((), (), s32[]{:S(2)}) async-start(), calls=%async_computation.14 | async-start | bytes 6488064 | tf_op jit(solution)/shard_map/all_gather | solution.py:170
  361.5 399.9 %reduce-scatter.13.cloned.1.call-start = ((), (), s32[]{:S(2)}) async-start(), calls=%async_computation.17 | async-start | bytes 7864320 | tf_op jit(solution)/shard_map/reduce_scatter | solution.py:244
  704.8 88.7 %all-gather.29.cloned.1.call-start = ((), (), s32[]{:S(2)}) async-start(), calls=%async_computation.18 | async-start | bytes 3932160 | tf_op jit(solution)/shard_map/all_gather | solution.py:251
  764.8 105.9 %all-gather.33.cloned.1.call-start = ((), (), s32[]{:S(2)}) async-start(), calls=%async_computation.25 | async-start | bytes 1179648 | tf_op jit(solution)/shard_map/all_gather | solution.py:37
  813.5 236.9 %reduce-scatter.23.cloned.1.call-start = ((), (), s32[]{:S(2)}) async-start(), calls=%async_computation.23 | async-start | bytes 12976128 | tf_op jit(solution)/shard_map/reduce_scatter | solution.py:122
  825.0 316.4 %reduce-scatter.19.cloned.1.call-start = ((), (), s32[]{:S(2)}) async-start(), calls=%async_computation.21 | async-start | bytes 4718592 | tf_op jit(solution)/shard_map/reduce_scatter | solution.py:308
  853.7 348.4 %reduce-scatter.15.cloned.1.call-start = ((), (), s32[]{:S(2)}) async-start(), calls=%async_computation.19 | async-start | bytes 7864320 | tf_op jit(solution)/shard_map/reduce_scatter | solution.py:299
  916.1 346.8 %reduce-scatter.11.cloned.1.call-start = ((), (), s32[]{:S(2)}) async-start(), calls=%async_computation.15 | async-start | bytes 7864320 | tf_op jit(solution)/shard_map/reduce_scatter | solution.py:231
  925.8 715.6 %reduce-scatter.21.cloned.1.call-start = ((), (), s32[]{:S(2)}) async-start(), calls=%async_computation.22 | async-start | bytes 25952256 | tf_op jit(solution)/shard_map/reduce_scatter | solution.py:121
  942.5 985.1 %reduce-scatter.17.cloned.1.call-start = ((), (), s32[]{:S(2)}) async-start(), calls=%async_computation.20 | async-start | bytes 18874368 | tf_op jit(solution)/shard_map/reduce_scatter | solution.py:307
  971.4 170.0 %copy-start.27 = (f32[512,256]{1,0:T(8,128)S(1)}, f32[512,256]{1,0:T(8,128)}, u32[]{:S(2)}) copy-start(f32[512,256]{1,0:T(8,128)} %param.33) | copy-start | bytes 1572868
  971.4 170.0 %copy-start.32 = (f32[512,256]{1,0:T(8,128)S(1)}, f32[512,256]{1,0:T(8,128)}, u32[]{:S(2)}) copy-start(f32[512,256]{1,0:T(8,128)} %param.37) | copy-start | bytes 1572868
  1055.7 146.4 %copy-start.35 = (f32[192]{0:T(256)S(1)}, f32[192]{0:T(256)}, u32[]{:S(2)}) copy-start(f32[192]{0:T(256)} %copy-done.34) | copy-start | bytes 2308
  1144.0 118.9 %copy-start.10 = (bf16[192,2048]{1,0:T(8,128)(2,1)S(1)}, bf16[192,2048]{1,0:T(8,128)(2,1)}, u32[]{:S(2)}) copy-start(bf16[192,2048]{1,0:T(8,128)(2,1)} %param.29) | copy-start | bytes 2359300
  1144.0 118.9 %copy-start.38 = (f32[192]{0:T(256)S(1)}, f32[192]{0:T(256)}, u32[]{:S(2)}) copy-start(f32[192]{0:T(256)} %copy-done.37) | copy-start | bytes 2308
  1656.0 271.6 %copy-start.3 = (f32[4,256,512]{1,2,0:T(8,128)S(1)}, f32[4,256,512]{1,2,0:T(8,128)}, u32[]{:S(2)}) copy-start(f32[4,256,512]{1,2,0:T(8,128)} %copy-done.2) | copy-start | bytes 6291460
  (37 other events, 323.8 us)
Sparse Core Ops, SparseCore 0:
  11.0 31.2 all-gather.14
  44.9 125.3 all-gather.16
  193.0 47.4 all-gather.30
  243.0 49.6 all-gather.18
  298.8 56.5 reduce-scatter.8
  358.3 163.6 all-gather.22
  524.2 26.7 all-gather.20
  552.6 28.5 all-gather.26
  583.9 93.5 all-gather.24
  704.9 56.5 reduce-scatter.12
  764.9 28.5 all-gather.28
  813.6 41.2 all-gather.32
  858.5 191.8 reduce-scatter.22
  1053.8 87.5 reduce-scatter.18
  1144.0 58.1 reduce-scatter.14
  1204.5 58.3 reduce-scatter.10
  1267.2 374.2 reduce-scatter.20
  1645.6 281.9 reduce-scatter.16
where the time goes:
time: 1960 us; the launch traced here: 1950 us
  waiting for transfers between devices  1560 us (80%)
  matrix products  151 us (8%)
  other arithmetic  84.5 us (4%)
  local copies, waits for them, and re-layouts  84 us (4%)
  blocking collectives  52.6 us (3%)
    reduce_scatter x1, waiting for transfers between devices, sum_feed(): lax.psum_scatter(glu_grad, 'seq', scatter_dimension=1, tiled=True)  374 us
    reduce_scatter x1, waiting for transfers between devices, local(): lax.psum_scatter(mixer_grad, 'seq', scatter_dimension=1, tiled=True)  268 us
    all_gather x1, waiting for transfers between devices, local(): lax.all_gather(glu_weight.astype(bf16), 'seq', axis=1, tiled=True)  160 us
    all_gather x1, waiting for transfers between devices, local(): lax.all_gather(mixer_weight.astype(bf16), 'seq', axis=1, tiled=True)  128 us
    all_gather x1, waiting for transfers between devices, local(): lax.all_gather(down_weight.astype(bf16), 'seq', axis=1, tiled=True)  96.4 us
    reduce_scatter x1, waiting for transfers between devices, local(): lax.psum_scatter(output_grad, 'seq', scatter_dimension=1, tiled=True)  85.7 us
    reduce_scatter x1, waiting for transfers between devices, sum_feed(): lax.psum_scatter(down_grad, 'seq', scatter_dimension=1, tiled=True)  79 us
    reduce_scatter x1, waiting for transfers between devices, local(): lax.psum_scatter(jnp.dot(product, down_full, preferred_element_type=f32),...  59 us
  transfers between devices with their start and end apart: 18, of which 17 were waited for; matrix products, arithmetic and copies ran while one was open for 12% of the time, Pallas kernels for 0%

commit v1 on v0

v1 whole, which is shorter than its diff:
```python
import jax
import jax.numpy as jnp
from jax import lax
from jax.sharding import PartitionSpec as P

D = 2048
HD = 128
BLK = 256
STEP = 10


NORM_EPS = 1e-06
BETA_ONE = 0.9
BETA_TWO = 0.95
ADAM_EPS = 1e-08
WEIGHT_DECAY = 0.1
LEARN_RATE = 0.02

bf16 = jnp.bfloat16
f32 = jnp.float32


class Ring:
    def __init__(self, size):
        self.size = size
        self.order = [*range(0, size, 2), *range(size - 1, 0, -2)]
        after = {a: self.order[(i + 1) % size] for i, a in enumerate(self.order)}
        self.perms = ([(a, b) for a, b in after.items()], [(b, a) for a, b in after.items()])
        self.arrived = ([], [])

    def place(self):
        spot = [0] * self.size
        for i, a in enumerate(self.order):
            spot[a] = i
        here = jnp.asarray(spot, jnp.int32)[lax.axis_index("seq")]
        table = jnp.asarray(self.order, jnp.int32)
        half = self.size // 2
        self.owner = {
            off: table[lax.rem(here + off + self.size, self.size)]
            for off in range(1 - half, half + 1)
        }

    def send(self, value, way):
        past = self.arrived[way]
        if len(past) >= 2:
            value, _ = lax.optimization_barrier((value, past[-2]))
        value = lax.ppermute(value, "seq", self.perms[way])
        past.append(value)
        return value


def spread(ring, shard, axis, cut):
    size, half = ring.size, ring.size // 2
    wide = shard.shape[axis]
    shape = list(shard.shape)
    shape[axis] = wide * size
    whole = jnp.zeros(shape, shard.dtype)

    def put(whole, piece, off, shift=None):
        at = [0] * shard.ndim
        at[axis] = ring.owner[off] * wide
        if shift is not None:
            at[cut] = at[cut] + shift
        return lax.dynamic_update_slice(whole, piece, at)

    whole = put(whole, shard, 0)
    up = down = shard
    for k in range(1, half):
        up, down = ring.send(up, 0), ring.send(down, 1)
        whole = put(whole, up, -k)
        whole = put(whole, down, k)
        yield
    mid = shard.shape[cut] // 2
    first = lax.slice_in_dim(up, 0, mid, axis=cut)
    second = lax.slice_in_dim(down, mid, shard.shape[cut], axis=cut)
    first, second = ring.send(first, 0), ring.send(second, 1)
    whole = put(whole, first, half, 0)
    whole = put(whole, second, half, mid)
    return whole


def collect(ring, own, cut):
    half = ring.size // 2
    far = own(half).astype(bf16)
    mid = far.shape[cut] // 2
    up = ring.send(lax.slice_in_dim(far, 0, mid, axis=cut), 0)
    down = ring.send(lax.slice_in_dim(far, mid, far.shape[cut], axis=cut), 1)
    yield
    for k in range(half - 1, 0, -1):
        above, below = own(k), own(-k)
        pads = [(0, 0)] * above.ndim
        if k == half - 1:
            pads[cut] = (0, above.shape[cut] - mid)
            up = jnp.pad(up, pads)
            pads[cut] = (mid, 0)
            down = jnp.pad(down, pads)
        up = ring.send((above + up.astype(f32)).astype(bf16), 0)
        down = ring.send((below + down.astype(f32)).astype(bf16), 1)
        if k > 1:
            yield
    return own(0) + up.astype(f32) + down.astype(f32)


def in_turn(*work):
    done = [None] * len(work)
    left = list(range(len(work)))
    while left:
        for i in list(left):
            try:
                next(work[i])
            except StopIteration as end:
                done[i] = end.value
                left.remove(i)
    return done


def layout(seq_lengths, first_block, block_count):
    blocks = (seq_lengths + BLK - 1) // BLK
    count = seq_lengths.shape[0]
    earlier = jnp.arange(count)[:, None] > jnp.arange(count)[None, :]
    starts = jnp.sum(jnp.where(earlier, blocks[None, :], 0), axis=1)
    block_index = first_block + jnp.arange(block_count, dtype=jnp.int32)
    begins = starts[None, :] == block_index[:, None]
    keep_flags = 1.0 - jnp.any(begins, axis=1).astype(jnp.float32)
    owner_index = jnp.sum((starts[None, :] <= block_index[:, None]).astype(jnp.int32), axis=1) - 1
    chosen = jnp.arange(count, dtype=jnp.int32)[None, :] == owner_index[:, None]
    own_start = jnp.sum(jnp.where(chosen, starts[None, :], 0), axis=1)
    own_length = jnp.sum(jnp.where(chosen, seq_lengths[None, :], 0), axis=1)
    position = (block_index - own_start)[:, None] * BLK + jnp.arange(BLK, dtype=jnp.int32)[None, :]
    token_mask = position < own_length[:, None]
    return (keep_flags, token_mask.reshape(block_count * BLK))


def normalize(values):
    norm_scale = lax.rsqrt(jnp.mean(values * values, axis=-1, keepdims=True) + NORM_EPS)
    return (values * norm_scale, norm_scale)


def norm_back(normed, norm_scale, incoming):
    return norm_scale * (incoming - normed * jnp.mean(incoming * normed, axis=-1, keepdims=True))


def silu_slope(values):
    sigmoid_v = jax.nn.sigmoid(values)
    return sigmoid_v * (1.0 + values * (1.0 - sigmoid_v))


def build_decays(cumulative):
    per_head = jnp.transpose(cumulative, (0, 2, 1))
    rows_in = per_head.shape[2]
    causal = jnp.arange(rows_in)[:, None] >= jnp.arange(rows_in)[None, :]
    log_gaps = jnp.minimum(per_head[:, :, :, None] - per_head[:, :, None, :], 0.0)
    return jnp.where(causal, jnp.exp(log_gaps), 0.0)


def adamw_step(weight, first, second, gradient):
    first_new = BETA_ONE * first + (1.0 - BETA_ONE) * gradient
    second_new = BETA_TWO * second + (1.0 - BETA_TWO) * gradient * gradient
    fix_one = 1.0 - BETA_ONE**STEP
    fix_two = 1.0 - BETA_TWO**STEP
    update = first_new / fix_one / (jnp.sqrt(second_new / fix_two) + ADAM_EPS)
    return (weight - LEARN_RATE * (update + WEIGHT_DECAY * weight), first_new, second_new)


def mm(spec, a, b):
    return jnp.einsum(spec, a, b, preferred_element_type=f32)


def scatter_rows(value):
    return lax.psum_scatter(value.astype(bf16), "tp", scatter_dimension=0, tiled=True).astype(f32)


def gather_rows(value):
    return lax.all_gather(value, "tp", axis=0, tiled=True)


def solution(mesh):
    size = mesh.shape["seq"]

    def local(
        inputs,
        out_grad,
        seq_lengths,
        log_decay,
        mixer_weight,
        output_weight,
        glu_weight,
        down_weight,
        mixer_first,
        output_first,
        glu_first,
        down_first,
        mixer_second,
        output_second,
        glu_second,
        down_second,
    ):
        group_rows = log_decay.shape[0]
        heads_here = log_decay.shape[1]
        blocks_here = group_rows // BLK
        width_here = heads_here * HD
        ring = Ring(size)
        ring.place()
        seq_place = lax.axis_index("seq")
        keep_flags, token_mask = layout(seq_lengths, seq_place * blocks_here, blocks_here)
        mask_col = token_mask[:, None]
        mask_float = mask_col.astype(f32)

        mixer_low = mixer_weight.astype(bf16)
        output_low = output_weight.astype(bf16)
        glu_low = glu_weight.astype(bf16)
        down_low = down_weight.astype(bf16)

        inputs_f = inputs.astype(f32)
        normed_one, scale_one = normalize(inputs_f)
        rows_one = gather_rows(normed_one.astype(bf16))
        grad_rows = gather_rows(out_grad)

        key_full, value_full = in_turn(
            spread(ring, mixer_low[1], 0, 0), spread(ring, mixer_low[2], 0, 0)
        )
        query_full, gate_full = in_turn(
            spread(ring, mixer_low[0], 0, 0), spread(ring, mixer_low[3], 0, 0)
        )
        (output_full,) = in_turn(spread(ring, output_low, 1, 0))
        left_full, right_full = in_turn(
            spread(ring, glu_low[0], 0, 0), spread(ring, glu_low[1], 0, 0)
        )
        mid = down_low.shape[0] // 2
        down_parts = in_turn(
            spread(ring, down_low[:mid], 1, 0), spread(ring, down_low[mid:], 1, 0)
        )

        key_pre = mm("td,dc->tc", rows_one, key_full)
        value_pre = mm("td,dc->tc", rows_one, value_full)
        query_pre = mm("td,dc->tc", rows_one, query_full)
        gate_u = mm("td,dc->tc", rows_one, gate_full)
        zero_low = jnp.zeros((), bf16)
        queries = jax.nn.silu(query_pre).astype(bf16)
        keys_all = jnp.where(mask_col, jax.nn.silu(key_pre).astype(bf16), zero_low)
        values_all = jnp.where(mask_col, value_pre.astype(bf16), zero_low)
        block_shape = (blocks_here, BLK, heads_here, HD)
        query_blocks = queries.reshape(block_shape)
        key_blocks = keys_all.reshape(block_shape)
        value_blocks = values_all.reshape(block_shape)
        lower = (jnp.arange(BLK)[:, None] >= jnp.arange(BLK)[None, :]).astype(f32)
        cumulative = jnp.einsum(
            "ts,bsh->bth",
            lower,
            log_decay.reshape(blocks_here, BLK, heads_here),
            precision=lax.Precision.HIGHEST,
        )
        block_ends = cumulative[:, -1, :]
        exp_cum = jnp.exp(cumulative)[..., None]
        exp_tail = jnp.exp(block_ends[:, None, :] - cumulative)[..., None]
        decays = build_decays(cumulative)
        scaled_k = (key_blocks * exp_tail).astype(bf16)
        state_terms = mm("bshe,bshf->bhef", scaled_k, value_blocks)
        factors = keep_flags[:, None] * jnp.exp(block_ends)

        state = state_terms[0]
        factor = factors[0]
        for j in range(1, blocks_here):
            state = factors[j][:, None, None] * state + state_terms[j]
            factor = factor * factors[j]
        all_states = lax.all_gather(state.astype(bf16), "seq")
        all_factors = lax.all_gather(factor, "seq")
        place = jnp.arange(size)

        def reach(between):
            picked = jnp.where(between[:, :, None], all_factors[None, :, :], 1.0)
            total = picked[:, 0]
            for i in range(1, size):
                total = total * picked[:, i]
            return total

        from_before = jnp.where(
            (place < seq_place)[:, None],
            reach((place[None, :] > place[:, None]) & (place[None, :] < seq_place)),
            0.0,
        )
        from_after = jnp.where(
            (place > seq_place)[:, None],
            reach((place[None, :] < place[:, None]) & (place[None, :] > seq_place)),
            0.0,
        )
        entering = jnp.sum(from_before[:, :, None, None] * all_states.astype(f32), axis=0)
        used = []
        for j in range(blocks_here):
            used.append(keep_flags[j] * entering)
            entering = factors[j][:, None, None] * entering + state_terms[j]
        used_low = jnp.stack(used).astype(bf16)

        scores = mm("bthe,bshe->bhts", query_blocks, key_blocks)
        block_probs = (scores * decays).astype(bf16)
        inner_part = mm("bhts,bshf->bthf", block_probs, value_blocks)
        scaled_q = (query_blocks * exp_cum).astype(bf16)
        outer_part = mm("bthe,bhef->bthf", scaled_q, used_low)
        mixer_out = (inner_part + outer_part).reshape(group_rows, width_here)
        squares = lax.psum(jnp.sum(mixer_out * mixer_out, axis=1), "tp")
        mixer_scale = lax.rsqrt(squares / D + NORM_EPS)[:, None]
        mixer_normed = mixer_out * mixer_scale
        joined = (mixer_normed * gate_u).astype(bf16)
        branch = scatter_rows(mm("tc,cd->td", joined, output_full))
        middle = inputs_f + branch
        normed_two, scale_two = normalize(middle)
        rows_two = gather_rows(normed_two.astype(bf16))

        gate_left = mm("td,dc->tc", rows_two, left_full)
        gate_right = mm("td,dc->tc", rows_two, right_full)
        product = (gate_left * gate_right).astype(bf16)
        down_full = jnp.concatenate(down_parts, axis=0)
        product_grad = mm("td,cd->tc", grad_rows, down_full)
        left_grad = (product_grad * gate_right).astype(bf16)
        right_grad = (product_grad * gate_left).astype(bf16)
        two_grad = scatter_rows(
            mm("tc,dc->td", left_grad, left_full) + mm("tc,dc->td", right_grad, right_full)
        )
        middle_grad = out_grad.astype(f32) + norm_back(normed_two, scale_two, two_grad)
        branch_grad = gather_rows(middle_grad.astype(bf16))

        feed_in, _ = lax.optimization_barrier((product, branch_grad))
        feed_out = scatter_rows(mm("tc,cd->td", feed_in, down_full))
        block_out = (middle + feed_out).astype(bf16)

        def columns(rows, off):
            wide = rows.shape[1] // size
            return lax.dynamic_slice_in_dim(rows, ring.owner[off] * wide, wide, axis=1)

        down_sums = in_turn(
            collect(ring, lambda off: mm("tc,td->cd", product[:, :mid], columns(grad_rows, off)), 0),
            collect(ring, lambda off: mm("tc,td->cd", product[:, mid:], columns(grad_rows, off)), 0),
        )
        glu_sums = in_turn(
            collect(ring, lambda off: mm("td,tc->dc", columns(rows_two, off), left_grad), 0),
            collect(ring, lambda off: mm("td,tc->dc", columns(rows_two, off), right_grad), 0),
        )

        joined_grad = mm("td,cd->tc", branch_grad, output_full)
        gate_grad = (joined_grad * mixer_normed).astype(bf16)
        output_sum, gate_sum = in_turn(
            collect(ring, lambda off: mm("tc,td->cd", joined, columns(branch_grad, off)), 0),
            collect(ring, lambda off: mm("td,tc->dc", columns(rows_one, off), gate_grad), 0),
        )
        normed_grad = joined_grad * gate_u
        row_dots = lax.psum(jnp.sum(normed_grad * mixer_normed, axis=1), "tp")
        mixed_grad = (
            mixer_scale * (normed_grad - mixer_normed * (row_dots / D)[:, None])
        ).astype(bf16)
        grad_blocks = mixed_grad.reshape(block_shape)
        kept_terms = keep_flags[:, None, None, None] * mm("bthe,bthf->bhef", scaled_q, grad_blocks)
        back = kept_terms[blocks_here - 1]
        for j in range(blocks_here - 2, -1, -1):
            back = factors[j][:, None, None] * back + kept_terms[j]
        all_back = lax.all_gather(back.astype(bf16), "seq")
        leaving = jnp.sum(from_after[:, :, None, None] * all_back.astype(f32), axis=0)
        state_grads = [None] * blocks_here
        for j in range(blocks_here - 1, -1, -1):
            state_grads[j] = leaving
            leaving = factors[j][:, None, None] * leaving + kept_terms[j]
        state_low = jnp.stack(state_grads).astype(bf16)
        value_dots = mm("bthf,bshf->bhts", grad_blocks, value_blocks)
        score_grad = (value_dots * decays).astype(bf16)
        query_grad = (
            mm("bhts,bshe->bthe", score_grad, key_blocks)
            + mm("bthf,bhef->bthe", grad_blocks, used_low) * exp_cum
        )
        key_grad = (
            mm("bhts,bthe->bshe", score_grad, query_blocks)
            + mm("bshf,bhef->bshe", value_blocks, state_low) * exp_tail
        )
        value_grad = mm("bhts,bthf->bshf", block_probs, grad_blocks) + mm(
            "bshe,bhef->bshf", scaled_k, state_low
        )
        query_back = (query_grad.reshape(group_rows, width_here) * silu_slope(query_pre)).astype(
            bf16
        )
        key_back = (
            key_grad.reshape(group_rows, width_here) * mask_float * silu_slope(key_pre)
        ).astype(bf16)
        value_back = (value_grad.reshape(group_rows, width_here) * mask_float).astype(bf16)

        query_sum, key_sum, value_sum = in_turn(
            collect(ring, lambda off: mm("td,tc->dc", columns(rows_one, off), query_back), 0),
            collect(ring, lambda off: mm("td,tc->dc", columns(rows_one, off), key_back), 0),
            collect(ring, lambda off: mm("td,tc->dc", columns(rows_one, off), value_back), 0),
        )
        one_grad = scatter_rows(
            mm("tc,dc->td", query_back, query_full)
            + mm("tc,dc->td", key_back, key_full)
            + mm("tc,dc->td", value_back, value_full)
            + mm("tc,dc->td", gate_grad, gate_full)
        )
        input_grad = middle_grad + norm_back(normed_one, scale_one, one_grad)

        mixer_sum = jnp.stack([query_sum, key_sum, value_sum, gate_sum])
        glu_sum = jnp.stack(glu_sums)
        down_sum = jnp.concatenate(down_sums, axis=0)
        mixer_new, mixer_first_new, mixer_second_new = adamw_step(
            mixer_weight, mixer_first, mixer_second, mixer_sum
        )
        output_new, output_first_new, output_second_new = adamw_step(
            output_weight, output_first, output_second, output_sum
        )
        glu_new, glu_first_new, glu_second_new = adamw_step(
            glu_weight, glu_first, glu_second, glu_sum
        )
        down_new, down_first_new, down_second_new = adamw_step(
            down_weight, down_first, down_second, down_sum
        )
        return (
            block_out,
            input_grad,
            mixer_new,
            output_new,
            glu_new,
            down_new,
            mixer_first_new,
            output_first_new,
            glu_first_new,
            down_first_new,
            mixer_second_new,
            output_second_new,
            glu_second_new,
            down_second_new,
        )

    rows = P(("seq", "tp"), None)
    deep, tall = P(None, "seq", "tp"), P("tp", "seq")
    weights = (deep, tall, deep, tall)
    in_specs = (rows, rows, P(), P("seq", "tp"), *weights * 3)
    out_specs = (rows, rows, *weights * 3)
    return jax.shard_map(local, mesh=mesh, in_specs=in_specs, out_specs=out_specs, check_vma=False)
```

time: 1960 us -> 875 us (0.45)
  waiting for transfers between devices: 1560 us -> 276 us
  starting transfers between devices: 1.11 us -> 162 us
  matrix products: 151 us -> 202 us
  other arithmetic: 84.5 us -> 45.9 us
  local copies, waits for them, and re-layouts: 84 us -> 119 us
  blocking collectives: 52.6 us -> 32.7 us
    reduce_scatter x8 -> x4, waiting for transfers between devices: 1030 us -> 2.9 us  [scatter_rows(): lax.psum_scatter(value.astype(bf16), 'tp', scatter_dimension=0, tiled=True)]
    all_gather x10 -> x6, waiting for transfers between devices: 526 us -> 33.1 us  [the longest x1 18.7 us: local(): all_back = lax.all_gather(back.astype(bf16), 'seq')]
    ppermute x0 -> x144, waiting for transfers between devices: none -> 239 us  [send(): value = lax.ppermute(value, 'seq', self.perms[way])]
    ppermute x0 -> x144, starting transfers between devices: none -> 161 us  [send(): value = lax.ppermute(value, 'seq', self.perms[way])]
    dynamic_update_slice x3 -> x79, local copies, waits for them, and re-layouts: 2.03 us -> 65.8 us  [put(): return lax.dynamic_update_slice(whole, piece, at)]
    dot_general x24 -> x101, matrix products: 151 us -> 202 us  [the longest x100 202 us: mm(): return jnp.einsum(spec, a, b, preferred_element_type=f32)]
    unnamed x2 -> x0, blocking collectives: 40.5 us -> none
    unnamed x104 -> x229, local copies, waits for them, and re-layouts: 46.1 us -> 11.8 us
  transfers between devices with their start and end apart: 18 -> 154, of which waited for: 17 -> 66; matrix products, arithmetic and copies ran while one was open for 12% -> 34% of each run, Pallas kernels for 0% -> 0%
where the time goes in v1:
time: 875 us; the launch traced here: 865 us
  waiting for transfers between devices  276 us (32%)
  matrix products  202 us (23%)
  starting transfers between devices  162 us (19%)
  local copies, waits for them, and re-layouts  119 us (14%)
  other arithmetic  45.9 us (5%)
  blocking collectives  32.7 us (4%)
  between operations  27.1 us (3%)
    ppermute x144, waiting for transfers between devices, send(): value = lax.ppermute(value, 'seq', self.perms[way])  239 us
    dot_general x100, matrix products, mm(): return jnp.einsum(spec, a, b, preferred_element_type=f32)  202 us
    ppermute x144, starting transfers between devices, send(): value = lax.ppermute(value, 'seq', self.perms[way])  161 us
    dynamic_update_slice x79, local copies, waits for them, and re-layouts, put(): return lax.dynamic_update_slice(whole, piece, at)  65.8 us
    all_gather x1, blocking collectives, local(): all_factors = lax.all_gather(factor, 'seq')  21 us
    all_gather x1, waiting for transfers between devices, local(): all_back = lax.all_gather(back.astype(bf16), 'seq')  18.7 us
  transfers between devices with their start and end apart: 154, of which 66 were waited for; matrix products, arithmetic and copies ran while one was open for 34% of the time, Pallas kernels for 0%

profile of v1, /device:TPU:0, one launch (start us, length us, event | category | flops | bytes accessed | tf_op | source)
XLA Modules:
  0.0 864.5 jit_solution(11890563274292297317)
XLA Ops:
  27.0 21.0 %all-gather = f32[8,1,4]{2,1,0:T(1,128)S(1)} all-gather(f32[1,1,4]{2,1,0:T(1,128)S(1)} %get-tuple-element.360), channel_id=1, replica_groups=mesh['seq'=8,'tp'=4] {'seq'}, dimensions={0}, use_global_device_ids=true | all-gather | bytes 144 | tf_op jit(solution)/shard_map/all_gather | solution.py:267
  187.0 14.4 %all-gather.10.cloned.1.call-done = bf16[8,4,128,128]{3,2,1,0:T(8,128)(2,1)} async-done(((bf16[1,4,128,128]{3,2,1,0:T(8,128)(2,1)}), bf16[8,4,128,128]{3,2,1,0:T(8,128)(2,1)}) %all-gather.10.cloned.1.call-update) | async-done | bytes 1048592 | tf_op jit(solution)/shard_map/all_gather | solution.py:266
  245.6 8.5 collective-permute-done.40
  254.6 12.8 %collective-permute-start.43 = (bf16[256,1408]{1,0:T(8,128)(2,1)S(1)}, bf16[256,1408]{1,0:T(8,128)(2,1)S(1)}, u32[]{:S(2)}, u32[]{:S(2)}) collective-permute-start(bf16[256,1408]{1,0:T(8,128)(2,1)S(1)} %collective-permute-done.41), channel_id=1, source_target_pairs={{8,0},{16,8},{24,16},{28,24},{20,28},{12,20},{4,12},{0,4},{9,1},{1... | collective-permute-start | bytes 2162696 | tf_op jit(solution)/shard_map/ppermute | solution.py:47
  273.4 11.5 %collective-permute-done.42 = bf16[256,1408]{1,0:T(8,128)(2,1)S(1)} collective-permute-done((bf16[256,1408]{1,0:T(8,128)(2,1)S(1)}, bf16[256,1408]{1,0:T(8,128)(2,1)S(1)}, u32[]{:S(2)}, u32[]{:S(2)}) %collective-permute-start.42) | collective-permute-done | bytes 720928 | tf_op jit(solution)/shard_map/ppermute | solution.py:47
  288.9 11.6 %collective-permute-done.50 = bf16[256,1408]{1,0:T(8,128)(2,1)} collective-permute-done((bf16[256,1408]{1,0:T(8,128)(2,1)S(1)}, bf16[256,1408]{1,0:T(8,128)(2,1)}, u32[]{:S(2)}, u32[]{:S(2)}) %collective-permute-start.50) | collective-permute-done | bytes 720928 | tf_op jit(solution)/shard_map/ppermute | solution.py:47
  306.6 9.2 %collective-permute-done.44 = bf16[256,1408]{1,0:T(8,128)(2,1)S(1)} collective-permute-done((bf16[256,1408]{1,0:T(8,128)(2,1)S(1)}, bf16[256,1408]{1,0:T(8,128)(2,1)S(1)}, u32[]{:S(2)}, u32[]{:S(2)}) %collective-permute-start.44) | collective-permute-done | bytes 720928 | tf_op jit(solution)/shard_map/ppermute | solution.py:47
  402.2 9.8 %fusion.3 = f32[1408,768]{0,1:T(8,128)} fusion(bf16[768,2048]{1,0:T(8,128)(2,1)} %all-gather.14.cloned.1.call-done, bf16[704,2048]{1,0:T(8,128)(2,1)} %constant_dynamic-update-slice_fusion.78, bf16[704,2048]{1,0:T(8,128)(2,1)} %constant_dynamic-update-slice_fusion.79), kind=kOutput, calls=%fused_computation.10 | convolution fusion | flops 4440719360 | bytes 13238272 | tf_op jit(solution)/shard_map/td,cd->tc/dot_general | solution.py:166
  412.0 8.6 fusion.423
  420.6 9.0 %fusion = (bf16[768,1408]{1,0:T(8,128)(2,1)S(1)}, bf16[768,1408]{1,0:T(8,128)(2,1)S(1)}, bf16[768,1408]{1,0:T(8,128)(2,1)}) fusion(f32[1408,768]{0,1:T(8,128)S(1)} %copy-done.111, f32[768,1408]{1,0:T(8,128)S(1)} %fusion.423, bf16[768,2048]{1,0:T(8,128)(2,1)S(1)} %copy-done.14, bf16[2048,1408]{1,0:T(8,128)(2,1)} %constant_dynamic-update-slice_fusion.16), kind=kOutput, calls=%fused_computation.5 | convolution fusion | flops 4435673088 | bytes 24051712 | tf_op jit(solution)/shard_map/td,dc->tc/dot_general | solution.py:166
  429.6 7.9 fusion.424
  437.5 9.2 %add_convert_fusion.1 = bf16[768,2048]{1,0:T(8,128)(2,1)} fusion(f32[768,2048]{1,0:T(8,128)S(1)} %fusion.424, bf16[768,1408]{1,0:T(8,128)(2,1)S(1)} %get-tuple-element.314, bf16[2048,1408]{1,0:T(8,128)(2,1)} %constant_dynamic-update-slice_fusion.25), kind=kOutput, calls=%fused_computation.1 | convolution fusion | flops 4432330752 | bytes 17367040 | tf_op jit(solution)/shard_map/tc,dc->td/dot_general | solution.py:166
  505.5 12.8 %collective-permute-done.75 = bf16[704,256]{1,0:T(8,128)(2,1)S(1)} collective-permute-done((bf16[704,256]{1,0:T(8,128)(2,1)S(1)}, bf16[704,256]{1,0:T(8,128)(2,1)S(1)}, u32[]{:S(2)}, u32[]{:S(2)}) %collective-permute-start.75) | collective-permute-done | bytes 360480 | tf_op jit(solution)/shard_map/ppermute | solution.py:47
  525.8 9.3 %collective-permute-done.122 = bf16[128,1408]{1,0:T(8,128)(2,1)S(1)} collective-permute-done((bf16[128,1408]{1,0:T(8,128)(2,1)S(1)}, bf16[128,1408]{1,0:T(8,128)(2,1)S(1)}, u32[]{:S(2)}, u32[]{:S(2)}) %collective-permute-start.122) | collective-permute-done | bytes 360480 | tf_op jit(solution)/shard_map/ppermute | solution.py:47
  543.5 11.5 %collective-permute-done.123 = bf16[256,1408]{1,0:T(8,128)(2,1)S(1)} collective-permute-done((bf16[256,1408]{1,0:T(8,128)(2,1)S(1)}, bf16[256,1408]{1,0:T(8,128)(2,1)S(1)}, u32[]{:S(2)}, u32[]{:S(2)}) %collective-permute-start.123) | collective-permute-done | bytes 720928 | tf_op jit(solution)/shard_map/ppermute | solution.py:47
  560.4 10.0 %collective-permute-done.110 = bf16[256,1408]{1,0:T(8,128)(2,1)S(1)} collective-permute-done((bf16[256,1408]{1,0:T(8,128)(2,1)S(1)}, bf16[256,1408]{1,0:T(8,128)(2,1)S(1)}, u32[]{:S(2)}, u32[]{:S(2)}) %collective-permute-start.110) | collective-permute-done | bytes 720928 | tf_op jit(solution)/shard_map/ppermute | solution.py:47
  573.5 6.7 multiply_reduce_fusion.2
  580.3 6.0 psum.15
  617.9 18.7 %all-gather.18.cloned.1.call-done = bf16[8,4,128,128]{3,2,1,0:T(8,128)(2,1)} async-done(((bf16[1,4,128,128]{3,2,1,0:T(8,128)(2,1)}), bf16[8,4,128,128]{3,2,1,0:T(8,128)(2,1)}) %all-gather.18.cloned.1.call-update) | async-done | bytes 1048592 | tf_op jit(solution)/shard_map/all_gather | solution.py:355
  659.2 7.5 add_convert_fusion
  679.9 8.2 collective-permute-done.78
  692.3 11.3 %collective-permute-done.92 = bf16[256,1408]{1,0:T(8,128)(2,1)S(1)} collective-permute-done((bf16[256,1408]{1,0:T(8,128)(2,1)S(1)}, bf16[256,1408]{1,0:T(8,128)(2,1)S(1)}, u32[]{:S(2)}, u32[]{:S(2)}) %collective-permute-start.92) | collective-permute-done | bytes 720928 | tf_op jit(solution)/shard_map/ppermute | solution.py:47
  704.8 12.1 %collective-permute-done.79 = bf16[256,1408]{1,0:T(8,128)(2,1)S(1)} collective-permute-done((bf16[256,1408]{1,0:T(8,128)(2,1)S(1)}, bf16[256,1408]{1,0:T(8,128)(2,1)S(1)}, u32[]{:S(2)}, u32[]{:S(2)}) %collective-permute-start.79) | collective-permute-done | bytes 720928 | tf_op jit(solution)/shard_map/ppermute | solution.py:47
  730.0 9.2 %fusion.4 = bf16[768,2048]{1,0:T(8,128)(2,1)} fusion(bf16[768,1408]{1,0:T(8,128)(2,1)S(1)} %copy-done.110, bf16[704,2048]{1,0:T(8,128)(2,1)} %constant_dynamic-update-slice_fusion.78, bf16[704,2048]{1,0:T(8,128)(2,1)} %constant_dynamic-update-slice_fusion.79), kind=kOutput, calls=%fused_computation.12 | convolution fusion | flops 4442292224 | bytes 11075584 | tf_op jit(solution)/shard_map/tc,cd->td/dot_general | solution.py:166
  (818 shorter events, 580.7 us)
Async XLA Ops:
  7.2 141.4 %all-gather.8.cloned.1.call-start = ((), (), s32[]{:S(2)}) async-start(), calls=%async_computation.4 | async-start | bytes 3932160 | tf_op jit(solution)/shard_map/all_gather | solution.py:174
  10.0 51.6 %collective-permute-start.13 = (bf16[256,512]{1,0:T(8,128)(2,1)}, bf16[256,512]{1,0:T(8,128)(2,1)}, u32[]{:S(2)}, u32[]{:S(2)}) collective-permute-start(bf16[256,512]{1,0:T(8,128)(2,1)} %get-tuple-element.326), channel_id=1, source_target_pairs={{8,0},{16,8},{24,16},{28,24},{20,28},{12,20},{4,12},{0,4},{9,1},{1... | collective-permute-start | bytes 786440 | tf_op jit(solution)/shard_map/ppermute | solution.py:47
  13.0 48.6 %collective-permute-start.8 = (bf16[256,512]{1,0:T(8,128)(2,1)}, bf16[256,512]{1,0:T(8,128)(2,1)}, u32[]{:S(2)}, u32[]{:S(2)}) collective-permute-start(bf16[256,512]{1,0:T(8,128)(2,1)} %get-tuple-element.326), channel_id=1, source_target_pairs={{0,8},{8,16},{16,24},{24,28},{28,20},{20,12},{12,4},{4,0},{1,9},{9... | collective-permute-start | bytes 786440 | tf_op jit(solution)/shard_map/ppermute | solution.py:47
  13.2 50.5 %collective-permute-start = (bf16[256,512]{1,0:T(8,128)(2,1)}, bf16[256,512]{1,0:T(8,128)(2,1)}, u32[]{:S(2)}, u32[]{:S(2)}) collective-permute-start(bf16[256,512]{1,0:T(8,128)(2,1)} %get-tuple-element.329), channel_id=1, source_target_pairs={{0,8},{8,16},{16,24},{24,28},{28,20},{20,12},{12,4},{4,0},{1,9},{9... | collective-permute-start | bytes 786440 | tf_op jit(solution)/shard_map/ppermute | solution.py:47
  15.1 48.6 %collective-permute-start.1 = (bf16[256,512]{1,0:T(8,128)(2,1)}, bf16[256,512]{1,0:T(8,128)(2,1)}, u32[]{:S(2)}, u32[]{:S(2)}) collective-permute-start(bf16[256,512]{1,0:T(8,128)(2,1)} %get-tuple-element.329), channel_id=1, source_target_pairs={{8,0},{16,8},{24,16},{28,24},{20,28},{12,20},{4,12},{0,4},{9,1},{1... | collective-permute-start | bytes 786440 | tf_op jit(solution)/shard_map/ppermute | solution.py:47
  17.1 184.3 %all-gather.10.cloned.1.call-start = ((), (), s32[]{:S(2)}) async-start(), calls=%async_computation.5 | async-start | bytes 1179648 | tf_op jit(solution)/shard_map/all_gather | solution.py:266
  163.7 156.6 %reduce-scatter.5.cloned.1.call-start = ((), (), s32[]{:S(2)}) async-start(), calls=%async_computation.6 | async-start | bytes 3932160 | tf_op jit(solution)/shard_map/reduce_scatter | solution.py:170
  226.2 176.0 %all-gather.14.cloned.1.call-start = ((), (), s32[]{:S(2)}) async-start(), calls=%async_computation.8 | async-start | bytes 3932160 | tf_op jit(solution)/shard_map/all_gather | solution.py:174
  226.8 185.3 %all-gather.12.cloned.1.call-start = ((), (), s32[]{:S(2)}) async-start(), calls=%async_computation.7 | async-start | bytes 3932160 | tf_op jit(solution)/shard_map/all_gather | solution.py:174
  254.0 30.9 %collective-permute-start.42 = (bf16[256,1408]{1,0:T(8,128)(2,1)S(1)}, bf16[256,1408]{1,0:T(8,128)(2,1)S(1)}, u32[]{:S(2)}, u32[]{:S(2)}) collective-permute-start(bf16[256,1408]{1,0:T(8,128)(2,1)S(1)} %collective-permute-done.40), channel_id=1, source_target_pairs={{0,8},{8,16},{16,24},{24,28},{28,20},{20,12},{12,4},{4,0},{1,9},{9... | collective-permute-start | bytes 2162696 | tf_op jit(solution)/shard_map/ppermute | solution.py:47
  254.6 30.9 %collective-permute-start.43 = (bf16[256,1408]{1,0:T(8,128)(2,1)S(1)}, bf16[256,1408]{1,0:T(8,128)(2,1)S(1)}, u32[]{:S(2)}, u32[]{:S(2)}) collective-permute-start(bf16[256,1408]{1,0:T(8,128)(2,1)S(1)} %collective-permute-done.41), channel_id=1, source_target_pairs={{8,0},{16,8},{24,16},{28,24},{20,28},{12,20},{4,12},{0,4},{9,1},{1... | collective-permute-start | bytes 2162696 | tf_op jit(solution)/shard_map/ppermute | solution.py:47
  269.5 31.0 %collective-permute-start.50 = (bf16[256,1408]{1,0:T(8,128)(2,1)S(1)}, bf16[256,1408]{1,0:T(8,128)(2,1)}, u32[]{:S(2)}, u32[]{:S(2)}) collective-permute-start(bf16[256,1408]{1,0:T(8,128)(2,1)S(1)} %collective-permute-done.48), channel_id=1, source_target_pairs={{0,8},{8,16},{16,24},{24,28},{28,20},{20,12},{12,4},{4,0},{1,9},{9... | collective-permute-start | bytes 2162696 | tf_op jit(solution)/shard_map/ppermute | solution.py:47
  270.1 31.0 %collective-permute-start.51 = (bf16[256,1408]{1,0:T(8,128)(2,1)S(1)}, bf16[256,1408]{1,0:T(8,128)(2,1)}, u32[]{:S(2)}, u32[]{:S(2)}) collective-permute-start(bf16[256,1408]{1,0:T(8,128)(2,1)S(1)} %collective-permute-done.49), channel_id=1, source_target_pairs={{8,0},{16,8},{24,16},{28,24},{20,28},{12,20},{4,12},{0,4},{9,1},{1... | collective-permute-start | bytes 2162696 | tf_op jit(solution)/shard_map/ppermute | solution.py:47
  284.9 30.9 %collective-permute-start.44 = (bf16[256,1408]{1,0:T(8,128)(2,1)S(1)}, bf16[256,1408]{1,0:T(8,128)(2,1)S(1)}, u32[]{:S(2)}, u32[]{:S(2)}) collective-permute-start(bf16[256,1408]{1,0:T(8,128)(2,1)S(1)} %collective-permute-done.42), channel_id=1, source_target_pairs={{0,8},{8,16},{16,24},{24,28},{28,20},{20,12},{12,4},{4,0},{1,9},{9... | collective-permute-start | bytes 2162696 | tf_op jit(solution)/shard_map/ppermute | solution.py:47
  285.5 31.6 %collective-permute-start.45 = (bf16[256,1408]{1,0:T(8,128)(2,1)S(1)}, bf16[256,1408]{1,0:T(8,128)(2,1)S(1)}, u32[]{:S(2)}, u32[]{:S(2)}) collective-permute-start(bf16[256,1408]{1,0:T(8,128)(2,1)S(1)} %collective-permute-done.43), channel_id=1, source_target_pairs={{8,0},{16,8},{24,16},{28,24},{20,28},{12,20},{4,12},{0,4},{9,1},{1... | collective-permute-start | bytes 2162696 | tf_op jit(solution)/shard_map/ppermute | solution.py:47
  323.0 160.7 %reduce-scatter.7.cloned.1.call-start = ((), (), s32[]{:S(2)}) async-start(), calls=%async_computation.9 | async-start | bytes 3932160 | tf_op jit(solution)/shard_map/reduce_scatter | solution.py:170
  446.7 126.9 %all-gather.16.cloned.1.call-start = ((), (), s32[]{:S(2)}) async-start(), calls=%async_computation.10 | async-start | bytes 3932160 | tf_op jit(solution)/shard_map/all_gather | solution.py:174
  487.3 149.3 %all-gather.18.cloned.1.call-start = ((), (), s32[]{:S(2)}) async-start(), calls=%async_computation.12 | async-start | bytes 1179648 | tf_op jit(solution)/shard_map/all_gather | solution.py:355
  542.9 123.8 %collective-permute-start.77 = (bf16[256,1408]{1,0:T(8,128)(2,1)}, bf16[256,1408]{1,0:T(8,128)(2,1)}, u32[]{:S(2)}, u32[]{:S(2)}) collective-permute-start(bf16[256,1408]{1,0:T(8,128)(2,1)} %add_convert_fusion.14), channel_id=1, source_target_pairs={{0,8},{8,16},{16,24},{24,28},{28,20},{20,12},{12,4},{4,0},{1,9},{9... | collective-permute-start | bytes 2162696 | tf_op jit(solution)/shard_map/ppermute | solution.py:47
  556.7 112.8 %collective-permute-start.124 = (bf16[256,1408]{1,0:T(8,128)(2,1)}, bf16[256,1408]{1,0:T(8,128)(2,1)}, u32[]{:S(2)}, u32[]{:S(2)}) collective-permute-start(bf16[256,1408]{1,0:T(8,128)(2,1)} %add_convert_fusion.4), channel_id=1, source_target_pairs={{8,0},{16,8},{24,16},{28,24},{20,28},{12,20},{4,12},{0,4},{9,1},{1... | collective-permute-start | bytes 2162696 | tf_op jit(solution)/shard_map/ppermute | solution.py:47
  559.8 113.8 %collective-permute-start.91 = (bf16[256,1408]{1,0:T(8,128)(2,1)}, bf16[256,1408]{1,0:T(8,128)(2,1)}, u32[]{:S(2)}, u32[]{:S(2)}) collective-permute-start(bf16[256,1408]{1,0:T(8,128)(2,1)} %add_convert_fusion.10), channel_id=1, source_target_pairs={{0,8},{8,16},{16,24},{24,28},{28,20},{20,12},{12,4},{4,0},{1,9},{9... | collective-permute-start | bytes 2162696 | tf_op jit(solution)/shard_map/ppermute | solution.py:47
  572.2 104.5 %collective-permute-start.111 = (bf16[256,1408]{1,0:T(8,128)(2,1)}, bf16[256,1408]{1,0:T(8,128)(2,1)}, u32[]{:S(2)}, u32[]{:S(2)}) collective-permute-start(bf16[256,1408]{1,0:T(8,128)(2,1)} %add_convert_fusion.7), channel_id=1, source_target_pairs={{8,0},{16,8},{24,16},{28,24},{20,28},{12,20},{4,12},{0,4},{9,1},{1... | collective-permute-start | bytes 2162696 | tf_op jit(solution)/shard_map/ppermute | solution.py:47
  597.8 254.0 %reduce-scatter.11.cloned.1.call-start = ((), (), s32[]{:S(2)}) async-start(), calls=%async_computation.13 | async-start | bytes 3932160 | tf_op jit(solution)/shard_map/reduce_scatter | solution.py:170
  666.7 186.8 %reduce-scatter.9.cloned.1.call-start = ((), (), s32[]{:S(2)}) async-start(), calls=%async_computation.11 | async-start | bytes 3932160 | tf_op jit(solution)/shard_map/reduce_scatter | solution.py:170
  (244 other events, 3316.7 us)
Sparse Core Ops, SparseCore 0:
  17.2 30.2 all-gather.7
  163.8 37.5 all-gather.9
  226.3 36.9 reduce-scatter.4
  264.8 28.5 all-gather.13
  323.1 27.5 all-gather.11
  446.8 36.8 reduce-scatter.6
  487.4 28.5 all-gather.15
  597.9 38.6 all-gather.17
  666.8 36.7 reduce-scatter.10
  739.4 35.8 reduce-scatter.8

commit v2 on v1

v2 whole, which is shorter than its diff:
```python
import functools

import jax
import jax.numpy as jnp
from jax import lax
from jax.experimental import pallas as pl
from jax.experimental.pallas import tpu as pltpu
from jax.sharding import PartitionSpec as P

D = 2048
HD = 128
BLK = 256
STEP = 10


NORM_EPS = 1e-06
BETA_ONE = 0.9
BETA_TWO = 0.95
ADAM_EPS = 1e-08
WEIGHT_DECAY = 0.1
LEARN_RATE = 0.02

bf16 = jnp.bfloat16
f32 = jnp.float32


class Ring:
    def __init__(self, size):
        self.size = size
        self.half = size // 2
        self.order = [*range(0, size, 2), *range(size - 1, 0, -2)]
        after = {a: self.order[(i + 1) % size] for i, a in enumerate(self.order)}
        self.perms = ([(a, b) for a, b in after.items()], [(b, a) for a, b in after.items()])
        self.offsets = [0]
        for k in range(1, self.half):
            self.offsets += [-k, k]
        self.offsets.append(self.half)
        self.groups = []
        self.sent = []
        self.after = ()

    def place(self):
        size = self.size
        index = lax.axis_index("seq")
        here = jnp.where(index % 2 == 0, index // 2, size - 1 - index // 2)

        def device(spot):
            spot = lax.rem(spot + size, size)
            return jnp.where(spot < size // 2, 2 * spot, 2 * (size - 1 - spot) + 1)

        def rank(off):
            off = lax.rem(off + size, size)
            return jnp.where(off == 0, 0, jnp.where(off < size // 2, 2 * off, 2 * (size - off) - 1))

        self.into = [device(here + off) for off in self.offsets]
        spots = [a // 2 if a % 2 == 0 else size - 1 - a // 2 for a in range(size)]
        self.back = [rank(spot - here) for spot in spots]

    def pick(self, rows, places):
        wide = rows.shape[1] // self.size
        return jnp.concatenate(
            [lax.dynamic_slice_in_dim(rows, at * wide, wide, axis=1) for at in places], axis=1
        )

    def columns(self, rows, off):
        wide = rows.shape[1] // self.size
        at = self.offsets.index(off) * wide
        return rows[:, at : at + wide]

    def send(self, value, way):
        waits = [v for group in self.groups[-3:-1] for v in group]
        if waits or self.after:
            value = lax.optimization_barrier((value, *waits, *self.after))[0]
        self.sent.append(value)
        return lax.ppermute(value, "seq", self.perms[way])


def spread(ring, shard, side):
    pieces = [shard]
    ends = [shard, shard]
    for _ in range(1, ring.half):
        ends = [ring.send(end, way) for way, end in enumerate(ends)]
        pieces += ends
        yield ends
    far = ring.send(ends[side], side)
    pieces.append(far)
    yield [far]
    return pieces


def collect(ring, own, side):
    def add(parts, other):
        sums, at = [], 0
        for p in parts:
            sums.append(p + other[:, at : at + p.shape[1]].astype(f32))
            at += p.shape[1]
        return sums

    def low(parts):
        parts = [p.astype(bf16) for p in parts]
        return parts[0] if len(parts) == 1 else jnp.concatenate(parts, axis=1)

    ends = [None, None]
    ends[side] = ring.send(low(own(ring.half)), side)
    yield [ends[side]]
    for k in range(ring.half - 1, 0, -1):
        parts = [own(off) if end is None else add(own(off), end) for off, end in zip((k, -k), ends)]
        ends = [ring.send(low(p), way) for way, p in enumerate(parts)]
        yield ends
    return add(add(own(0), ends[0]), ends[1])


def turns(lanes, count, *after):
    for _ in range(count):
        for lane in lanes:
            lane.turn(*after)


def then(lanes, turn, *values):
    waits = [v for lane in lanes for v in lane.got[turn - 1]]
    out = lax.optimization_barrier((*values, *waits))[: len(values)]
    return out if len(values) > 1 else out[0]


def behind(lanes, turn, *values):
    waits = [v for lane in lanes for v in lane.gave[turn - 1]]
    out = lax.optimization_barrier((*values, *waits))[: len(values)]
    return out if len(values) > 1 else out[0]


class Line:
    def __init__(self, ring, work):
        self.ring = ring
        self.work = work
        self.got = []
        self.gave = []

    def turn(self, *after):
        self.ring.after = after
        before = len(self.ring.sent)
        self.got.append(next(self.work))
        self.ring.groups.append(self.got[-1])
        self.ring.after = ()
        self.gave.append(self.ring.sent[before:])

    def end(self):
        try:
            next(self.work)
        except StopIteration as end:
            return end.value
        raise ValueError("turns left")


def layout(seq_lengths, first_block, block_count):
    blocks = (seq_lengths + BLK - 1) // BLK
    count = seq_lengths.shape[0]
    earlier = jnp.arange(count)[:, None] > jnp.arange(count)[None, :]
    starts = jnp.sum(jnp.where(earlier, blocks[None, :], 0), axis=1)
    block_index = first_block + jnp.arange(block_count, dtype=jnp.int32)
    begins = starts[None, :] == block_index[:, None]
    keep_flags = 1.0 - jnp.any(begins, axis=1).astype(jnp.float32)
    owner_index = jnp.sum((starts[None, :] <= block_index[:, None]).astype(jnp.int32), axis=1) - 1
    chosen = jnp.arange(count, dtype=jnp.int32)[None, :] == owner_index[:, None]
    own_start = jnp.sum(jnp.where(chosen, starts[None, :], 0), axis=1)
    own_length = jnp.sum(jnp.where(chosen, seq_lengths[None, :], 0), axis=1)
    position = (block_index - own_start)[:, None] * BLK + jnp.arange(BLK, dtype=jnp.int32)[None, :]
    token_mask = position < own_length[:, None]
    return (keep_flags, token_mask.reshape(block_count * BLK))


def normalize(values):
    norm_scale = lax.rsqrt(jnp.mean(values * values, axis=-1, keepdims=True) + NORM_EPS)
    return (values * norm_scale, norm_scale)


def norm_back(normed, norm_scale, incoming):
    return norm_scale * (incoming - normed * jnp.mean(incoming * normed, axis=-1, keepdims=True))


MEBI = 2**20


def dot(a, b):
    return lax.dot_general(a, b, (((1,), (0,)), ((), ())), preferred_element_type=f32)


def dot_t(a, b):
    return lax.dot_general(a, b, (((1,), (1,)), ((), ())), preferred_element_type=f32)


def t_dot(a, b):
    return lax.dot_general(a, b, (((0,), (0,)), ((), ())), preferred_element_type=f32)


class Rows:
    def __init__(self, array):
        self.array = array


class Scalars:
    def __init__(self, array):
        self.array = array


def by_block(body, inputs, weights, outs, scratch=(), backward=False, vmem=60, flops=0):
    count = next(i.array.shape[0] for i in inputs if isinstance(i, Rows)) // BLK
    pieces = [p for stack in weights for group, _, _ in stack for p in group]
    turn = (lambda i: count - 1 - i) if backward else (lambda i: i)

    def spec(shape):
        part = shape[0] // count
        return pl.BlockSpec(
            (part, *shape[1:]), lambda i: (turn(i), *[0] * (len(shape) - 1))
        )

    def whole(shape):
        return pl.BlockSpec(shape, lambda i: (0,) * len(shape))

    in_specs, arrays = [], []
    for i in inputs:
        if isinstance(i, Rows):
            in_specs.append(spec(i.array.shape))
            arrays.append(i.array)
        elif isinstance(i, Scalars):
            in_specs.append(pl.BlockSpec(memory_space=pltpu.SMEM))
            arrays.append(i.array)
        else:
            in_specs.append(whole(i.shape))
            arrays.append(i)
    in_specs += [pl.BlockSpec(memory_space=pl.ANY)] * len(pieces)
    stacks = [
        (sum(p.shape[0] for p in stack[0][0]), sum(end - start for _, start, end in stack))
        for stack in weights
    ]

    def kernel(*refs):
        ins, refs = refs[: len(arrays)], refs[len(arrays) :]
        sources, refs = refs[: len(pieces)], refs[len(pieces) :]
        results, refs = refs[: len(outs)], refs[len(outs) :]
        held, refs = refs[: len(stacks)], refs[len(stacks) :]
        extra, sems = refs[: len(scratch)], refs[len(scratch) :]
        at = pl.program_id(0)

        if pieces:

            @pl.when(at == 0)
            def _():
                copies = []
                k = 0
                for parts, stack in zip(weights, held, strict=True):
                    column = 0
                    for group, start, end in parts:
                        row = 0
                        for p in group:
                            copies.append(
                                pltpu.make_async_copy(
                                    sources[k].at[:, start:end],
                                    stack.at[
                                        pl.ds(row, p.shape[0]), pl.ds(column, end - start)
                                    ],
                                    sems[0].at[k],
                                )
                            )
                            row += p.shape[0]
                            k += 1
                        column += end - start
                for c in copies:
                    c.start()
                for c in copies:
                    c.wait()

        body(at, turn(at), ins, held, results, extra)

    out = pl.pallas_call(
        kernel,
        grid=(count,),
        in_specs=in_specs,
        out_specs=[spec(shape) if cut else whole(shape) for shape, _, cut in outs],
        out_shape=[jax.ShapeDtypeStruct(shape, kind) for shape, kind, _ in outs],
        scratch_shapes=[
            *[pltpu.VMEM(shape, bf16) for shape in stacks],
            *scratch,
            *([pltpu.SemaphoreType.DMA((len(pieces),))] if pieces else []),
        ],
        compiler_params=pltpu.CompilerParams(
            dimension_semantics=("arbitrary",), vmem_limit_bytes=vmem * MEBI
        ),
        cost_estimate=pl.CostEstimate(
            flops=int(flops * COST), bytes_accessed=0, transcendentals=0
        ),
    )(*arrays, *pieces)
    return out


def enter(ring, inputs, out_grad):
    rows, width = inputs.shape
    wide = width // ring.size
    if wide % 128:
        here = ring.pick(inputs, ring.into)
        normed, scale = normalize(here.astype(f32))
        return normed.astype(bf16), here, ring.pick(out_grad, ring.into), scale

    def kernel(into, in_ref, grad_ref, normed_ref, here_ref, grad_here_ref, scale_ref):
        values = in_ref[...].astype(f32)
        scale = lax.rsqrt(jnp.mean(values * values, axis=-1, keepdims=True) + NORM_EPS)
        scale_ref[...] = scale
        for i in range(ring.size):
            at = pl.ds(pl.multiple_of(into[i] * wide, 128), wide)
            to = slice(i * wide, (i + 1) * wide)
            part = in_ref[:, at]
            here_ref[:, to] = part
            normed_ref[:, to] = (part.astype(f32) * scale).astype(bf16)
            grad_here_ref[:, to] = grad_ref[:, at]

    return pl.pallas_call(
        kernel,
        in_specs=[pl.BlockSpec(memory_space=pltpu.SMEM)] + [pl.BlockSpec(inputs.shape)] * 2,
        out_shape=[jax.ShapeDtypeStruct(inputs.shape, bf16)] * 3
        + [jax.ShapeDtypeStruct((rows, 1), f32)],
        compiler_params=pltpu.CompilerParams(vmem_limit_bytes=60 * MEBI),
    )(jnp.stack(ring.into), inputs, out_grad)


def leave(ring, kind, function, *values):
    rows, width = values[0].shape
    wide = width // ring.size
    if wide % 128:
        return ring.pick(function(*values).astype(kind), ring.back)

    def kernel(into, *refs):
        result = function(*[r[...] for r in refs[:-1]]).astype(kind)
        for i in range(ring.size):
            at = pl.ds(pl.multiple_of(into[i] * wide, 128), wide)
            refs[-1][:, at] = result[:, i * wide : (i + 1) * wide]

    return pl.pallas_call(
        kernel,
        in_specs=[pl.BlockSpec(memory_space=pltpu.SMEM)] + [pl.BlockSpec(v.shape) for v in values],
        out_shape=jax.ShapeDtypeStruct((rows, width), kind),
        compiler_params=pltpu.CompilerParams(vmem_limit_bytes=60 * MEBI),
    )(jnp.stack(ring.into), *values)


def head(ref, h):
    return ref[:, h * HD : (h + 1) * HD]


def decay_of(column, row):
    causal = lax.broadcasted_iota(jnp.int32, (BLK, BLK), 0) >= lax.broadcasted_iota(
        jnp.int32, (BLK, BLK), 1
    )
    return jnp.where(causal, jnp.exp(jnp.minimum(column - row, 0.0)), 0.0)


def silu_slope(values):
    sigmoid_v = jax.nn.sigmoid(values)
    return sigmoid_v * (1.0 + values * (1.0 - sigmoid_v))


def keys_kernel(heads, at, block, ins, held, outs, extra):
    rows, mask, tail, factors, ending = ins
    pre_out, keys_out, values_out, scaled_out, terms_out, message_out = outs
    (state,) = extra
    wide = heads * HD

    @pl.when(at == 0)
    def _():
        state[...] = jnp.zeros_like(state)
        message_out[wide:, :] = ending[...]

    pre = dot(rows[...], held[0][...])
    key_pre, value_pre = pre[:, :wide], pre[:, wide:]
    pre_out[...] = key_pre
    keep = mask[...]
    keys = (jax.nn.silu(key_pre).astype(bf16) * keep).astype(bf16)
    values = (value_pre.astype(bf16) * keep).astype(bf16)
    keys_out[...] = keys
    values_out[...] = values
    for h in range(heads):
        part = slice(h * HD, (h + 1) * HD)
        scaled = (keys[:, part].astype(f32) * tail[:, h : h + 1]).astype(bf16)
        scaled_out[:, part] = scaled
        term = t_dot(scaled, values[:, part])
        terms_out[part, :] = term
        renewed = factors[block, h] * state[part, :] + term
        state[part, :] = renewed
        message_out[part, :] = renewed.astype(bf16)


def queries_kernel(heads, at, block, ins, held, outs, extra):
    rows, keys, values, column, row = ins
    pre_out, gate_out, queries_out, scaled_out, probs_out, inner_out = outs
    wide = heads * HD
    both = dot(rows[...], held[0][...])
    query_pre = both[:, :wide]
    pre_out[...] = query_pre
    gate_out[...] = both[:, wide:]
    queries = jax.nn.silu(query_pre).astype(bf16)
    queries_out[...] = queries
    for h in range(heads):
        here = queries[:, h * HD : (h + 1) * HD]
        sums = column[:, h : h + 1]
        scaled_out[:, h * HD : (h + 1) * HD] = (here.astype(f32) * jnp.exp(sums)).astype(bf16)
        decays = decay_of(sums, row[0, h : h + 1, :])
        probs = (dot_t(here, head(keys, h)) * decays).astype(bf16)
        probs_out[:, h * BLK : (h + 1) * BLK] = probs
        inner_out[:, h * HD : (h + 1) * HD] = dot(probs, head(values, h))


def lanes(values):
    total = values[:, :HD]
    for i in range(1, values.shape[1] // HD):
        total = total + values[:, i * HD : (i + 1) * HD]
    return total


def states_kernel(heads, at, block, ins, held, outs, extra):
    inner, scaled, terms, message, reach, factors, keep = ins
    mixed_out, squares_out, used_out = outs
    (state,) = extra
    size = reach.shape[0]

    @pl.when(at == 0)
    def _():
        for h in range(heads):
            total = reach[0, h] * message[0, h * HD : (h + 1) * HD, :].astype(f32)
            for i in range(1, size):
                total = total + reach[i, h] * message[i, h * HD : (h + 1) * HD, :].astype(f32)
            state[h * HD : (h + 1) * HD, :] = total

    parts = []
    for h in range(heads):
        now = state[h * HD : (h + 1) * HD, :]
        used = (keep[block] * now).astype(bf16)
        used_out[h * HD : (h + 1) * HD, :] = used
        state[h * HD : (h + 1) * HD, :] = factors[block, h] * now + terms[h * HD : (h + 1) * HD, :]
        parts.append(head(inner, h) + dot(head(scaled, h), used))
    mixed = jnp.concatenate(parts, axis=1)
    mixed_out[...] = mixed
    squares_out[...] = lanes(mixed * mixed)


def branch_kernel(at, block, ins, held, outs, extra):
    mixed, gate, scale = ins
    joined_out, branch_out = outs
    joined = (mixed[...] * scale[...] * gate[...]).astype(bf16)
    joined_out[...] = joined
    branch_out[...] = dot_t(joined, held[0][...]).astype(bf16)


def gates_kernel(at, block, ins, held, outs, extra):
    (rows,) = ins
    left_out, right_out, product_out = outs
    hidden = left_out.shape[1]
    gates = dot(rows[...], held[0][...])
    left, right = gates[:, :hidden], gates[:, hidden:]
    left_out[...] = left
    right_out[...] = right
    product_out[...] = (left * right).astype(bf16)


def gates_back_kernel(at, block, ins, held, outs, extra):
    rows, left, right = ins
    (both_out,) = outs
    hidden = left.shape[1]
    product_grad = dot(rows[...], held[0][...])
    both_out[:, :hidden] = (product_grad * right[...]).astype(bf16)
    both_out[:, hidden:] = (product_grad * left[...]).astype(bf16)


def back_kernel(at, block, ins, held, outs, extra):
    total = dot_t(ins[0][...], held[0][...])
    for i, stack in zip(ins[1:], held[1:], strict=True):
        total = total + dot_t(i[...], stack[...])
    outs[0][...] = total.astype(bf16)


def joined_back_kernel(at, block, ins, held, outs, extra):
    rows, mixed, gate, scale = ins
    gate_out, inward_out, dots_out = outs
    joined_grad = dot(rows[...], held[0][...])
    normed = mixed[...] * scale[...]
    gate_out[...] = (joined_grad * normed).astype(bf16)
    inward = joined_grad * gate[...]
    inward_out[...] = inward
    dots_out[...] = lanes(inward * normed)


def mixed_back_kernel(heads, at, block, ins, held, outs, extra):
    inward, mixed, scale, dots, scaled, factors, keep = ins
    grad_out, kept_out, back_out = outs
    (state,) = extra
    normed = mixed[...] * scale[...]
    grad = (scale[...] * (inward[...] - normed * dots[...])).astype(bf16)
    grad_out[...] = grad

    @pl.when(at == 0)
    def _():
        state[...] = jnp.zeros_like(state)

    for h in range(heads):
        part = slice(h * HD, (h + 1) * HD)
        kept = keep[block] * t_dot(head(scaled, h), grad[:, part])
        kept_out[part, :] = kept
        renewed = factors[block, h] * state[part, :] + kept
        state[part, :] = renewed
        back_out[part, :] = renewed.astype(bf16)


def scores_back_kernel(heads, at, block, ins, held, outs, extra):
    grad, keys, values, queries, probs, used, query_pre, column, row = ins
    query_out, key_out, value_out = outs
    for h in range(heads):
        part = slice(h * HD, (h + 1) * HD)
        here = grad[:, part]
        sums = column[:, h : h + 1]
        score = (dot_t(here, values[:, part]) * decay_of(sums, row[0, h : h + 1, :])).astype(bf16)
        query_grad = dot(score, keys[:, part]) + dot_t(here, used[part, :]) * jnp.exp(sums)
        query_out[:, part] = (query_grad * silu_slope(query_pre[:, part])).astype(bf16)
        key_out[:, part] = t_dot(score, queries[:, part])
        value_out[:, part] = t_dot(probs[:, h * BLK : (h + 1) * BLK], here)


def states_back_kernel(heads, at, block, ins, held, outs, extra):
    key_grad, value_grad, query, gate, values, scaled, kept, message = ins[:8]
    key_pre, mask, tail, reach, factors = ins[8:]
    pair_out, other_out = outs
    (state,) = extra
    size = reach.shape[0]
    wide = heads * HD

    @pl.when(at == 0)
    def _():
        for h in range(heads):
            total = reach[0, h] * message[0, h * HD : (h + 1) * HD, :].astype(f32)
            for i in range(1, size):
                total = total + reach[i, h] * message[i, h * HD : (h + 1) * HD, :].astype(f32)
            state[h * HD : (h + 1) * HD, :] = total

    keep = mask[...]
    for h in range(heads):
        part = slice(h * HD, (h + 1) * HD)
        now = state[part, :]
        low = now.astype(bf16)
        key = key_grad[:, part] + dot_t(values[:, part], low) * tail[:, h : h + 1]
        pair_out[:, part] = (key * keep * silu_slope(key_pre[:, part])).astype(bf16)
        value = value_grad[:, part] + dot(scaled[:, part], low)
        pair_out[:, wide + h * HD : wide + (h + 1) * HD] = (value * keep).astype(bf16)
        state[part, :] = factors[block, h] * now + kept[part, :]
    other_out[:, :wide] = query[...]
    other_out[:, wide:] = gate[...]


COST = 0.0


def mm(spec, a, b):
    return jnp.einsum(spec, a, b, preferred_element_type=f32)


def scatter_rows(value):
    return lax.psum_scatter(value, "tp", scatter_dimension=0, tiled=True)


def gather_rows(value):
    return lax.all_gather(value, "tp", axis=0, tiled=True)


def adamw_step(weight, first, second, gradient):
    first_new = BETA_ONE * first + (1.0 - BETA_ONE) * gradient
    second_new = BETA_TWO * second + (1.0 - BETA_TWO) * gradient * gradient
    fix_one = 1.0 - BETA_ONE**STEP
    fix_two = 1.0 - BETA_TWO**STEP
    update = first_new / fix_one / (jnp.sqrt(second_new / fix_two) + ADAM_EPS)
    return (weight - LEARN_RATE * (update + WEIGHT_DECAY * weight), first_new, second_new)


def adamw_across(weight, first, second, gradient):
    rows, columns = weight.shape
    part = 128

    def kernel(w, m, v, g, w_out, m_out, v_out):
        results = adamw_step(w[...], m[...], v[...], g[...].T)
        for ref, value in zip((w_out, m_out, v_out), results, strict=True):
            ref[...] = value

    here = pl.BlockSpec((part, columns), lambda i: (i, 0))
    return pl.pallas_call(
        kernel,
        grid=(rows // part,),
        in_specs=[here] * 3 + [pl.BlockSpec((columns, part), lambda i: (0, i))],
        out_specs=[here] * 3,
        out_shape=[jax.ShapeDtypeStruct(weight.shape, f32)] * 3,
        compiler_params=pltpu.CompilerParams(vmem_limit_bytes=60 * MEBI),
    )(weight, first, second, gradient)


def solution(mesh):
    size = mesh.shape["seq"]

    def local(
        inputs,
        out_grad,
        seq_lengths,
        log_decay,
        mixer_weight,
        output_weight,
        glu_weight,
        down_weight,
        mixer_first,
        output_first,
        glu_first,
        down_first,
        mixer_second,
        output_second,
        glu_second,
        down_second,
    ):
        rows = log_decay.shape[0]
        heads = log_decay.shape[1]
        blocks = rows // BLK
        wide = heads * HD
        hidden = down_weight.shape[0]
        ring = Ring(size)
        ring.place()
        half = ring.half
        seq_place = lax.axis_index("seq")
        keep_flags, token_mask = layout(seq_lengths, seq_place * blocks, blocks)
        mask_col = token_mask[:, None].astype(f32)

        output_low = output_weight.astype(bf16).T
        down_low = down_weight.astype(bf16).T
        pair, part = 2 * wide, wide // 2
        cut = hidden // 256 * 128
        mixer_lanes = [
            jnp.concatenate(
                [mixer_weight[i].astype(bf16), mixer_weight[j].astype(bf16), output_low[:, a:b]], axis=1
            )
            for i, j, a, b in ((1, 2, 0, part), (0, 3, part, wide))
        ]
        mixer = [Line(ring, spread(ring, low, i)) for i, low in enumerate(mixer_lanes)]
        glu = [Line(ring, spread(ring, glu_weight[i].astype(bf16), i)) for i in range(2)]
        down = [
            Line(ring, spread(ring, low, i))
            for i, low in enumerate((down_low[:, :cut], down_low[:, cut:]))
        ]

        rows_one_here, inputs_here, out_grad_here, scale_one = enter(ring, inputs, out_grad)
        rows_one = gather_rows(rows_one_here)
        grad_rows = gather_rows(out_grad_here)

        lower = (jnp.arange(BLK)[:, None] >= jnp.arange(BLK)[None, :]).astype(f32)
        cumulative = jnp.einsum(
            "ts,bsh->bth",
            lower,
            log_decay.reshape(blocks, BLK, heads),
            precision=lax.Precision.HIGHEST,
        )
        block_ends = cumulative[:, -1, :]
        tail = jnp.exp(block_ends[:, None, :] - cumulative).reshape(rows, heads)
        column = cumulative.reshape(rows, heads)
        row = jnp.transpose(cumulative, (0, 2, 1))
        factors = keep_flags[:, None] * jnp.exp(block_ends)

        turns(mixer, half)
        mixer_full = [lane.end() for lane in mixer]
        pair_stack, other_stack = [[(full, 0, pair)] for full in mixer_full]
        output_stack = [(full, pair, pair + part) for full in mixer_full]
        turns(glu, half)
        turns(down, half - 1)

        state_shape = (blocks * wide, HD)
        factor = factors[0]
        for j in range(1, blocks):
            factor = factor * factors[j]
        first = factor.astype(bf16)
        second = (factor - first.astype(f32)).astype(bf16)
        third = (factor - first.astype(f32) - second.astype(f32)).astype(bf16)
        ending = jnp.pad(jnp.stack([first, second, third]), ((0, 13), (0, HD - heads)))
        key_pre, keys, values, scaled_k, terms, message = by_block(
            functools.partial(keys_kernel, heads),
            [
                Rows(then(mixer, half, rows_one)),
                Rows(mask_col),
                Rows(tail),
                Scalars(factors),
                ending,
            ],
            [pair_stack],
            [
                ((rows, wide), f32, True),
                ((rows, wide), bf16, True),
                ((rows, wide), bf16, True),
                ((rows, wide), bf16, True),
                (state_shape, f32, True),
                ((wide + 16, HD), bf16, False),
            ],
            [pltpu.VMEM((wide, HD), f32)],
            flops=2 * rows * D * 2 * wide,
        )
        message, grad_rows = then(glu[:1], 1, message, grad_rows)
        message = lax.all_gather(message, "seq")
        all_factors = jnp.sum(message[:, wide : wide + 3, :heads].astype(f32), axis=1)
        place = jnp.arange(size)

        def reach(between):
            picked = jnp.where(between[:, :, None], all_factors[None, :, :], 1.0)
            total = picked[:, 0]
            for i in range(1, size):
                total = total * picked[:, i]
            return total

        from_before = jnp.where(
            (place < seq_place)[:, None],
            reach((place[None, :] > place[:, None]) & (place[None, :] < seq_place)),
            0.0,
        )
        from_after = jnp.where(
            (place > seq_place)[:, None],
            reach((place[None, :] < place[:, None]) & (place[None, :] > seq_place)),
            0.0,
        )
        query_pre, gate_u, queries, scaled_q, probs, inner = by_block(
            functools.partial(queries_kernel, heads),
            [Rows(rows_one), Rows(keys), Rows(values), Rows(column), Rows(row)],
            [other_stack],
            [
                ((rows, wide), f32, True),
                ((rows, wide), f32, True),
                ((rows, wide), bf16, True),
                ((rows, wide), bf16, True),
                ((rows, heads * BLK), bf16, True),
                ((rows, wide), f32, True),
            ],
            flops=2 * rows * D * 2 * wide,
        )
        inner = then(glu[1:], 1, inner)
        message = then(glu[:1], 2, message)
        mixer_out, squares, used = by_block(
            functools.partial(states_kernel, heads),
            [
                Rows(inner),
                Rows(scaled_q),
                Rows(terms),
                message,
                Scalars(from_before),
                Scalars(factors),
                Scalars(keep_flags),
            ],
            [],
            [((rows, wide), f32, True), ((rows, HD), f32, True), (state_shape, bf16, True)],
            [pltpu.VMEM((wide, HD), f32)],
            flops=2 * rows * D * wide // 4,
        )
        squares = then(glu[1:], 2, squares)
        squares = lax.psum(jnp.sum(squares, axis=1), "tp")
        mixer_scale = lax.rsqrt(squares / D + NORM_EPS)[:, None]
        joined, branch_here = by_block(
            branch_kernel,
            [Rows(mixer_out), Rows(gate_u), Rows(mixer_scale)],
            [output_stack],
            [((rows, wide), bf16, True), ((rows, D), bf16, True)],
            flops=2 * rows * D * wide,
        )
        branch = scatter_rows(then(glu[:1], 3, branch_here))
        middle = inputs_here.astype(f32) + then(glu, half, branch).astype(f32)
        normed_two, scale_two = normalize(middle)
        rows_two_here = normed_two.astype(bf16)
        rows_two = gather_rows(rows_two_here)
        rows_two = then(down, 1, rows_two)

        glu_stack = [(lane.end(), 0, hidden) for lane in glu]
        gate_left, gate_right, product = by_block(
            gates_kernel,
            [Rows(rows_two)],
            [glu_stack],
            [((rows, hidden), f32, True), ((rows, hidden), f32, True), ((rows, hidden), bf16, True)],
            flops=2 * rows * D * 2 * hidden,
        )

        product = then(down, half - 1, product)
        turns(down, 1)
        down_parts = [lane.end() for lane in down]
        down_stack = [(full, 0, full[0].shape[1]) for full in down_parts]
        down_total = [
            Line(
                ring,
                collect(
                    ring,
                    lambda off, cols=cols: [mm("td,tc->dc", ring.columns(grad_rows, off), cols)],
                    i,
                ),
            )
            for i, cols in enumerate((product[:, :cut], product[:, cut:]))
        ]
        turns(down_total, 1)
        (both_grads,) = by_block(
            gates_back_kernel,
            [Rows(grad_rows), Rows(gate_left), Rows(gate_right)],
            [down_stack],
            [((rows, 2 * hidden), bf16, True)],
            flops=2 * rows * D * hidden,
        )
        both_grads = then(down_total, 1, both_grads)
        turns(down_total, 1)
        glu_total = [
            Line(
                ring,
                collect(
                    ring,
                    lambda off, cols=cols: [mm("td,tc->dc", ring.columns(rows_two, off), cols)],
                    i,
                ),
            )
            for i, cols in enumerate((both_grads[:, :hidden], both_grads[:, hidden:]))
        ]
        turns(glu_total, 1)
        (two_here,) = by_block(
            back_kernel,
            [Rows(behind(glu_total, 1, both_grads))],
            [glu_stack],
            [((rows, D), bf16, True)],
            flops=2 * rows * D * 2 * hidden,
        )
        two_grad = scatter_rows(then(down_total, 2, two_here))
        turns(down_total, half - 2)
        two_grad = behind(down_total, half, then(down_total, half - 1, two_grad))
        middle_grad = out_grad_here.astype(f32) + norm_back(
            normed_two, scale_two, two_grad.astype(f32)
        )
        branch_grad = gather_rows(middle_grad.astype(bf16))
        turns(glu_total, 1)
        branch_grad = then(glu_total[:1], 2, branch_grad)

        gate_grad, inward, dots = by_block(
            joined_back_kernel,
            [Rows(branch_grad), Rows(mixer_out), Rows(gate_u), Rows(mixer_scale)],
            [output_stack],
            [((rows, wide), bf16, True), ((rows, wide), f32, True), ((rows, HD), f32, True)],
            flops=2 * rows * D * wide,
        )
        turns(glu_total, half - 2)
        dots = then(glu_total[1:], 2, dots)
        row_dots = (lax.psum(jnp.sum(dots, axis=1), "tp") / D)[:, None]
        mixed_grad, kept, back = by_block(
            functools.partial(mixed_back_kernel, heads),
            [
                Rows(inward),
                Rows(mixer_out),
                Rows(mixer_scale),
                Rows(row_dots),
                Rows(scaled_q),
                Scalars(factors),
                Scalars(keep_flags),
            ],
            [],
            [((rows, wide), bf16, True), (state_shape, f32, True), ((wide, HD), bf16, False)],
            [pltpu.VMEM((wide, HD), f32)],
            backward=True,
            flops=2 * rows * D * wide // 4,
        )
        all_back = lax.all_gather(back, "seq")
        (feed_here,) = by_block(
            back_kernel,
            [Rows(lax.optimization_barrier((product, back))[0])],
            [down_stack],
            [((rows, D), bf16, True)],
            flops=2 * rows * D * hidden,
        )
        feed_here = then(glu_total[:1], 3, feed_here)
        query_back, key_grad, value_grad = by_block(
            functools.partial(scores_back_kernel, heads),
            [
                Rows(lax.optimization_barrier((mixed_grad, feed_here))[0]),
                Rows(keys),
                Rows(values),
                Rows(queries),
                Rows(probs),
                Rows(used),
                Rows(query_pre),
                Rows(column),
                Rows(row),
            ],
            [],
            [((rows, wide), bf16, True), ((rows, wide), f32, True), ((rows, wide), f32, True)],
            flops=2 * rows * D * wide,
        )
        query_back = then(glu_total[1:], 3, query_back)
        feed_out = scatter_rows(lax.optimization_barrier((feed_here, all_back))[0])
        pair_grads, other_grads = by_block(
            functools.partial(states_back_kernel, heads),
            [
                Rows(key_grad),
                Rows(value_grad),
                Rows(query_back),
                Rows(gate_grad),
                Rows(values),
                Rows(scaled_k),
                Rows(kept),
                then(glu_total[:1], half, all_back),
                Rows(key_pre),
                Rows(mask_col),
                Rows(tail),
                Scalars(from_after),
                Scalars(factors),
            ],
            [],
            [((rows, pair), bf16, True), ((rows, pair), bf16, True)],
            [pltpu.VMEM((wide, HD), f32)],
            backward=True,
            flops=2 * rows * D * wide // 4,
        )
        pair_grads, other_grads = then(glu_total, half, pair_grads, other_grads)
        mixer_total = [
            Line(
                ring,
                collect(
                    ring,
                    lambda off, grads=grads, cols=cols: [
                        mm("td,tc->dc", ring.columns(rows_one, off), grads),
                        mm("td,tc->dc", ring.columns(branch_grad, off), cols),
                    ],
                    i,
                ),
            )
            for i, (grads, cols) in enumerate(
                ((pair_grads, joined[:, :part]), (other_grads, joined[:, part:]))
            )
        ]
        turns(mixer_total, half - 1)
        block_out = leave(ring, bf16, lambda a, b: a + b.astype(f32), middle, feed_out)
        (one_here,) = by_block(
            back_kernel,
            [Rows(behind(mixer_total, 1, pair_grads)), Rows(other_grads)],
            [pair_stack, other_stack],
            [((rows, D), bf16, True)],
            flops=2 * rows * D * 4 * wide,
        )
        one_grad = scatter_rows(then(mixer_total, 1, one_here))
        one_grad = then(mixer_total, half - 1, one_grad)
        input_grad = leave(
            ring,
            f32,
            lambda grad, rows, scale, incoming: (
                grad + norm_back(rows.astype(f32) * scale, scale, incoming.astype(f32))
            ),
            middle_grad,
            inputs_here,
            scale_one,
            one_grad,
        )

        turns(mixer_total, 1, block_out, input_grad)
        down_sum = jnp.concatenate([lane.end()[0] for lane in down_total], axis=1)
        glu_sum = jnp.stack([lane.end()[0] for lane in glu_total])
        (pair_sum, first_sum), (other_sum, second_sum) = [lane.end() for lane in mixer_total]
        output_sum = jnp.concatenate([first_sum, second_sum], axis=1)

        mixer_sum = jnp.stack(
            [other_sum[:, :wide], pair_sum[:, :wide], pair_sum[:, wide:], other_sum[:, wide:]]
        )
        mixer_new, mixer_first_new, mixer_second_new = adamw_step(
            mixer_weight, mixer_first, mixer_second, mixer_sum
        )
        output_new, output_first_new, output_second_new = adamw_across(
            output_weight, output_first, output_second, output_sum
        )
        glu_new, glu_first_new, glu_second_new = adamw_step(
            glu_weight, glu_first, glu_second, then(mixer_total, 2, glu_sum)
        )
        down_new, down_first_new, down_second_new = adamw_across(
            down_weight, down_first, down_second, then(mixer_total, 1, down_sum)
        )
        return (
            block_out,
            input_grad,
            mixer_new,
            output_new,
            glu_new,
            down_new,
            mixer_first_new,
            output_first_new,
            glu_first_new,
            down_first_new,
            mixer_second_new,
            output_second_new,
            glu_second_new,
            down_second_new,
        )

    rows = P(("seq", "tp"), None)
    deep, tall = P(None, "seq", "tp"), P("tp", "seq")
    weights = (deep, tall, deep, tall)
    in_specs = (rows, rows, P(), P("seq", "tp"), *weights * 3)
    out_specs = (rows, rows, *weights * 3)
    return jax.shard_map(local, mesh=mesh, in_specs=in_specs, out_specs=out_specs, check_vma=False)
```

time: 875 us -> 746 us (0.85)
  Pallas kernels: 0 us -> 152 us
  local copies, waits for them, and re-layouts: 119 us -> 12.8 us
  matrix products: 202 us -> 97.4 us
  starting transfers between devices: 162 us -> 89.2 us
  waiting for transfers between devices: 276 us -> 313 us
  blocking collectives: 32.7 us -> 12.2 us
  between operations: 27.1 us -> 16.2 us
    pallas_call x0 -> x18, Pallas kernels: none -> 152 us  [the longest x13 129 us: by_block(): pl.pallas_call(kernel, grid=(count,), in_specs=in_specs, out_specs=[spec(...]
    dot_general x100 -> x64, matrix products: 202 us -> 97.2 us  [mm(): return jnp.einsum(spec, a, b, preferred_element_type=f32)]
    ppermute x144 -> x84, starting transfers between devices: 161 us -> 88.6 us  [send(): return lax.ppermute(value, 'seq', self.perms[way])]
    ppermute x144 -> x84, waiting for transfers between devices: 239 us -> 306 us  [send(): return lax.ppermute(value, 'seq', self.perms[way])]
    dynamic_update_slice x79 -> x0, local copies, waits for them, and re-layouts: 65.8 us -> none  [put(): return lax.dynamic_update_slice(whole, piece, at)]
    all_gather x2, waiting for transfers between devices: 33 us -> 0.04 us  [the longest x1 0.02 us: local(): message = lax.all_gather(message, 'seq')]
    all_gather x1 -> x0, blocking collectives: 21 us -> none  [local(): all_factors = lax.all_gather(factor, 'seq')]
    concatenate x0 -> x18, other arithmetic: none -> 12.3 us  [the longest x14 9.01 us: low(): return parts[0] if len(parts) == 1 else jnp.concatenate(parts, axis=1)]
  transfers between devices with their start and end apart: 154 -> 94, of which waited for: 66 -> 57; matrix products, arithmetic and copies ran while one was open for 34% -> 18% of each run, Pallas kernels for 0% -> 17%
where the time goes in v2:
time: 746 us; the launch traced here: 736 us
  waiting for transfers between devices  313 us (42%)
  Pallas kernels  152 us (20%)
  matrix products  97.4 us (13%)
  starting transfers between devices  89.2 us (12%)
  other arithmetic  43.8 us (6%)
  between operations  16.2 us (2%)
  local copies, waits for them, and re-layouts  12.8 us (2%)
  blocking collectives  12.2 us (2%)
    ppermute x84, waiting for transfers between devices, send(): return lax.ppermute(value, 'seq', self.perms[way])  306 us
    pallas_call x13, Pallas kernels, by_block(): pl.pallas_call(kernel, grid=(count,), in_specs=in_specs, out_specs=[spec(...  129 us
    dot_general x64, matrix products, mm(): return jnp.einsum(spec, a, b, preferred_element_type=f32)  97.2 us
    ppermute x84, starting transfers between devices, send(): return lax.ppermute(value, 'seq', self.perms[way])  88.6 us
  transfers between devices with their start and end apart: 94, of which 57 were waited for; matrix products, arithmetic and copies ran while one was open for 18% of the time, Pallas kernels for 17%

profile of v2, /device:TPU:0, one launch (start us, length us, event | category | flops | bytes accessed | tf_op | source)
XLA Modules:
  0.0 735.8 jit_solution(15037892974878365101)
XLA Ops:
  20.2 10.8 %collective-permute-done.refs_6_.refs_4_.refs_5_.refs_3_ = bf16[256,1280]{1,0:T(8,128)(2,1)S(1)} collective-permute-done((bf16[256,1280]{1,0:T(8,128)(2,1)S(1)}, bf16[256,1280]{1,0:T(8,128)(2,1)S(1)}, u32[]{:S(2)}, u32[]{:S(2)}) %collective-permute-start) | collective-permute-done | bytes 655392 | tf_op jit(solution)/shard_map/ppermute | solution.py:75
  35.7 9.4 %collective-permute-done.3.refs_6_.refs_12_.refs_13_.refs_11_ = bf16[256,1280]{1,0:T(8,128)(2,1)} collective-permute-done((bf16[256,1280]{1,0:T(8,128)(2,1)S(1)}, bf16[256,1280]{1,0:T(8,128)(2,1)}, u32[]{:S(2)}, u32[]{:S(2)}) %collective-permute-start.3) | collective-permute-done | bytes 655392 | tf_op jit(solution)/shard_map/ppermute | solution.py:75
  49.3 9.7 %collective-permute-done.2.refs_8_.refs_6_.refs_7_.refs_5_ = bf16[256,1280]{1,0:T(8,128)(2,1)S(1)} collective-permute-done((bf16[256,1280]{1,0:T(8,128)(2,1)S(1)}, bf16[256,1280]{1,0:T(8,128)(2,1)S(1)}, u32[]{:S(2)}, u32[]{:S(2)}) %collective-permute-start.2) | collective-permute-done | bytes 655392 | tf_op jit(solution)/shard_map/ppermute | solution.py:75
  63.4 9.7 %collective-permute-done.7.refs_8_.refs_14_.refs_15_.refs_13_ = bf16[256,1280]{1,0:T(8,128)(2,1)S(1)} collective-permute-done((bf16[256,1280]{1,0:T(8,128)(2,1)}, bf16[256,1280]{1,0:T(8,128)(2,1)S(1)}, u32[]{:S(2)}, u32[]{:S(2)}) %collective-permute-start.7) | collective-permute-done | bytes 655392 | tf_op jit(solution)/shard_map/ppermute | solution.py:75
  77.3 9.8 %collective-permute-done.6.refs_10_.refs_8_.refs_9_.refs_7_ = bf16[256,1280]{1,0:T(8,128)(2,1)S(1)} collective-permute-done((bf16[256,1280]{1,0:T(8,128)(2,1)S(1)}, bf16[256,1280]{1,0:T(8,128)(2,1)S(1)}, u32[]{:S(2)}, u32[]{:S(2)}) %collective-permute-start.6) | collective-permute-done | bytes 655392 | tf_op jit(solution)/shard_map/ppermute | solution.py:75
  103.2 11.2 %collective-permute-done.10.refs_12_.refs_10_.refs_11_.refs_9_ = bf16[256,1280]{1,0:T(8,128)(2,1)S(1)} collective-permute-done((bf16[256,1280]{1,0:T(8,128)(2,1)S(1)}, bf16[256,1280]{1,0:T(8,128)(2,1)S(1)}, u32[]{:S(2)}, u32[]{:S(2)}) %collective-permute-start.10) | collective-permute-done | bytes 655392 | tf_op jit(solution)/shard_map/ppermute | solution.py:75
  119.9 9.4 %shard_map.264 = (f32[768,512]{1,0:T(8,128)}, bf16[768,512]{1,0:T(8,128)(2,1)}, bf16[768,512]{1,0:T(8,128)(2,1)}, bf16[768,512]{1,0:T(8,128)(2,1)}, f32[1536,128]{1,0:T(8,128)}, /*index=5*/bf16[528,128]{1,0:T(8,128)(2,1)}) custom-call(bf16[768,2048]{1,0:T(8,128)(2,1)} %all-gather.9.cloned.1.call-done.refs_0_, f32[768,1]{1,0:T(8,128)} %bitcast.82, ...), custom_call_target="tpu_custom_call" | custom-call | tf_op jit(solution)/shard_map/pallas_call | solution.py:274
  139.5 17.4 %collective-permute-done.14.refs_10_ = bf16[256,1408]{1,0:T(8,128)(2,1)S(1)} collective-permute-done((bf16[256,1408]{1,0:T(8,128)(2,1)S(1)}, bf16[256,1408]{1,0:T(8,128)(2,1)S(1)}, u32[]{:S(2)}, u32[]{:S(2)}) %collective-permute-start.14) | collective-permute-done | bytes 720928 | tf_op jit(solution)/shard_map/ppermute | solution.py:75
  161.3 18.7 %collective-permute-done.18.refs_4_ = bf16[256,1408]{1,0:T(8,128)(2,1)S(1)} collective-permute-done((bf16[256,1408]{1,0:T(8,128)(2,1)}, bf16[256,1408]{1,0:T(8,128)(2,1)S(1)}, u32[]{:S(2)}, u32[]{:S(2)}) %collective-permute-start.18) | collective-permute-done | bytes 720928 | tf_op jit(solution)/shard_map/ppermute | solution.py:75
  185.6 10.1 %shard_map.265 = (f32[768,512]{1,0:T(8,128)}, f32[768,512]{1,0:T(8,128)}, bf16[768,512]{1,0:T(8,128)(2,1)}, bf16[768,512]{1,0:T(8,128)(2,1)}, bf16[768,1024]{1,0:T(8,128)(2,1)}, /*index=5*/f32[768,512]{1,0:T(8,128)}) custom-call(bf16[768,2048]{1,0:T(8,128)(2,1)} %all-gather.9.cloned.1.call-done.refs_0_, bf16[768,512]{1,0:T(8,128)(2,1)} %get-tuple-element.174.refs_1_, ...), custom_call_target="tpu_custom_call" | custom-call | tf_op jit(solution)/shard_map/pallas_call | solution.py:274
  221.1 14.5 %collective-permute-done.25.refs_15_ = bf16[256,1408]{1,0:T(8,128)(2,1)S(1)} collective-permute-done((bf16[256,1408]{1,0:T(8,128)(2,1)}, bf16[256,1408]{1,0:T(8,128)(2,1)S(1)}, u32[]{:S(2)}, u32[]{:S(2)}) %collective-permute-start.25) | collective-permute-done | bytes 720928 | tf_op jit(solution)/shard_map/ppermute | solution.py:75
  237.7 13.4 %collective-permute-done.24.refs_8_ = bf16[256,1408]{1,0:T(8,128)(2,1)S(1)} collective-permute-done((bf16[256,1408]{1,0:T(8,128)(2,1)}, bf16[256,1408]{1,0:T(8,128)(2,1)S(1)}, u32[]{:S(2)}, u32[]{:S(2)}) %collective-permute-start.24) | collective-permute-done | bytes 720928 | tf_op jit(solution)/shard_map/ppermute | solution.py:75
  263.5 13.7 %collective-permute-done.28.refs_4_.refs_2_ = bf16[256,640]{1,0:T(8,128)(2,1)S(1)} collective-permute-done((bf16[256,640]{1,0:T(8,128)(2,1)S(1)}, bf16[256,640]{1,0:T(8,128)(2,1)S(1)}, u32[]{:S(2)}, u32[]{:S(2)}) %collective-permute-start.28) | collective-permute-done | bytes 327712 | tf_op jit(solution)/shard_map/ppermute | solution.py:75
  282.7 12.5 %collective-permute-done.32.refs_6_.refs_4_ = bf16[256,640]{1,0:T(8,128)(2,1)S(1)} collective-permute-done((bf16[256,640]{1,0:T(8,128)(2,1)S(1)}, bf16[256,640]{1,0:T(8,128)(2,1)S(1)}, u32[]{:S(2)}, u32[]{:S(2)}) %collective-permute-start.32) | collective-permute-done | bytes 327712 | tf_op jit(solution)/shard_map/ppermute | solution.py:75
  300.6 11.6 %collective-permute-done.34.refs_8_.refs_6_ = bf16[256,640]{1,0:T(8,128)(2,1)} collective-permute-done((bf16[256,640]{1,0:T(8,128)(2,1)S(1)}, bf16[256,640]{1,0:T(8,128)(2,1)}, u32[]{:S(2)}, u32[]{:S(2)}) %collective-permute-start.34) | collective-permute-done | bytes 327712 | tf_op jit(solution)/shard_map/ppermute | solution.py:75
  316.1 16.6 %shard_map.268 = (f32[768,1408]{1,0:T(8,128)}, f32[768,1408]{1,0:T(8,128)}, bf16[768,1408]{1,0:T(8,128)(2,1)}) custom-call(bf16[768,2048]{1,0:T(8,128)(2,1)} %all-gather.13.cloned.1.call-done.refs_0_, bf16[256,1408]{1,0:T(8,128)(2,1)} %get-tuple-element.183.refs_1_, bf16[256,1408]{1,0:T(8,128)(2,1)} %collective-permute-done.16.refs_2_, ...), custom_call_target="tpu_custom_call" | custom-call | tf_op jit(solution)/shard_map/pallas_call | solution.py:274
  343.0 12.8 %shard_map.269.refs_0_ = bf16[768,2816]{1,0:T(8,128)(2,1)} custom-call(bf16[768,2048]{1,0:T(8,128)(2,1)} %all-gather.11.cloned.1.call-done.refs_0_, f32[768,1408]{1,0:T(8,128)} %get-tuple-element.217.refs_1_, f32[768,1408]{1,0:T(8,128)} %get-tuple-element.218.refs_2_, bf16[256,640]{1,0:T(8,128)(2,1)} %copy-done.30, bf16[256,640]{1,0:T(8,128)(2,1)} %copy-done.56, ...), custom_call_target="tpu_custom_call" | custom-call | tf_op jit(solution)/shard_map/pallas_call | solution.py:274
  372.3 16.4 %shard_map.270 = bf16[768,2048]{1,0:T(8,128)(2,1)} custom-call(bf16[768,2816]{1,0:T(8,128)(2,1)} %shard_map.269.refs_0_, bf16[256,1408]{1,0:T(8,128)(2,1)} %get-tuple-element.183.refs_1_, bf16[256,1408]{1,0:T(8,128)(2,1)} %collective-permute-done.16.refs_2_, bf16[256,1408]{1,0:T(8,128)(2,1)} %collective-permute-done.17.refs_3_, ...), custom_call_target="tpu_custom_call" | custom-call | tf_op jit(solution)/shard_map/pallas_call | solution.py:274
  394.8 10.6 %collective-permute-done.48 = bf16[256,1408]{1,0:T(8,128)(2,1)S(1)} collective-permute-done((bf16[256,1408]{1,0:T(8,128)(2,1)}, bf16[256,1408]{1,0:T(8,128)(2,1)S(1)}, u32[]{:S(2)}, u32[]{:S(2)}) %collective-permute-start.48) | collective-permute-done | bytes 720928 | tf_op jit(solution)/shard_map/ppermute | solution.py:75
  512.4 9.4 %collective-permute-done.64 = bf16[256,1408]{1,0:T(8,128)(2,1)S(1)} collective-permute-done((bf16[256,1408]{1,0:T(8,128)(2,1)S(1)}, bf16[256,1408]{1,0:T(8,128)(2,1)S(1)}, u32[]{:S(2)}, u32[]{:S(2)}) %collective-permute-start.64) | collective-permute-done | bytes 720928 | tf_op jit(solution)/shard_map/ppermute | solution.py:75
  532.6 10.5 %shard_map.273 = bf16[768,2048]{1,0:T(8,128)(2,1)} custom-call(bf16[768,1408]{1,0:T(8,128)(2,1)} %get-tuple-element.251.refs_0_, bf16[256,640]{1,0:T(8,128)(2,1)} %copy-done.30, bf16[256,640]{1,0:T(8,128)(2,1)} %copy-done.56, bf16[256,640]{1,0:T(8,128)(2,1)} %copy-done.57, bf16[256,640]{1,0:T(8,128)(2,1)} %copy-done.58, bf16[256,640]{1,0:T(8,128)(2,1)} %copy-done.59, ...), custom_call_target="tpu_custom_call" | custom-call | tf_op jit(solution)/shard_map/pallas_call | solution.py:274
  593.8 13.0 %shard_map.277 = bf16[768,2048]{1,0:T(8,128)(2,1)} custom-call(bf16[768,1024]{1,0:T(8,128)(2,1)} %get-tuple-element.285.refs_0_, bf16[768,1024]{1,0:T(8,128)(2,1)} %get-tuple-element.283.refs_1_, bf16[256,1280]{1,0:T(8,128)(2,1)} %copy-done.4, bf16[256,1280]{1,0:T(8,128)(2,1)} %copy-done.8, bf16[256,1280]{1,0:T(8,128)(2,1)} %copy-done.9, ...), custom_call_target="tpu_custom_call" | custom-call | tf_op jit(solution)/shard_map/pallas_call | solution.py:274
  621.7 9.4 %shard_map.280 = (f32[1408,256]{1,0:T(8,128)}, f32[1408,256]{1,0:T(8,128)}, f32[1408,256]{1,0:T(8,128)}) custom-call(f32[1408,256]{1,0:T(8,128)} %w.3, f32[1408,256]{1,0:T(8,128)} %m.3, f32[1408,256]{1,0:T(8,128)} %v.3, f32[256,1408]{1,0:T(8,128)} %pad_maximum_fusion.2.g), custom_call_target="tpu_custom_call" | custom-call | tf_op jit(solution)/shard_map/pallas_call | solution.py:588
  655.7 16.4 %collective-permute-done.79 = bf16[256,1280]{1,0:T(8,128)(2,1)S(1)} collective-permute-done((bf16[256,1280]{1,0:T(8,128)(2,1)S(1)}, bf16[256,1280]{1,0:T(8,128)(2,1)S(1)}, u32[]{:S(2)}, u32[]{:S(2)}) %collective-permute-start.79) | collective-permute-done | bytes 655392 | tf_op jit(solution)/shard_map/ppermute | solution.py:75
  (520 shorter events, 422.6 us)
Async XLA Ops:
  7.2 112.6 %all-gather.9.cloned.1.call-start = ((), (), s32[]{:S(2)}) async-start(), calls=%async_computation.4 | async-start | bytes 3932160 | tf_op jit(solution)/shard_map/all_gather | solution.py:566
  11.1 123.1 %all-gather.11.cloned.1.call-start = ((), (), s32[]{:S(2)}) async-start(), calls=%async_computation.5 | async-start | bytes 3932160 | tf_op jit(solution)/shard_map/all_gather | solution.py:566
  11.9 183.9 %all-gather.17.cloned.1.call-start = ((), (), s32[]{:S(2)}) async-start(), calls=%async_computation.12 | async-start | bytes 1216512 | tf_op jit(solution)/shard_map/all_gather | solution.py:702
  134.2 120.7 %reduce-scatter.5.cloned.1.call-start = ((), (), s32[]{:S(2)}) async-start(), calls=%async_computation.6 | async-start | bytes 3932160 | tf_op jit(solution)/shard_map/reduce_scatter | solution.py:562
  136.3 43.7 %collective-permute-start.18 = (bf16[256,1408]{1,0:T(8,128)(2,1)}, bf16[256,1408]{1,0:T(8,128)(2,1)S(1)}, u32[]{:S(2)}, u32[]{:S(2)}) collective-permute-start(bf16[256,1408]{1,0:T(8,128)(2,1)} %collective-permute-done.16.refs_2_), channel_id=1, source_target_pairs={{0,8},{8,16},{16,24},{24,28},{28,20},{20,12},{12,4},{4,0},{1,9},{9... | collective-permute-start | bytes 2162696 | tf_op jit(solution)/shard_map/ppermute | solution.py:75
  137.9 45.6 %collective-permute-start.19 = (bf16[256,1408]{1,0:T(8,128)(2,1)}, bf16[256,1408]{1,0:T(8,128)(2,1)}, u32[]{:S(2)}, u32[]{:S(2)}) collective-permute-start(bf16[256,1408]{1,0:T(8,128)(2,1)} %collective-permute-done.17.refs_3_), channel_id=1, source_target_pairs={{8,0},{16,8},{24,16},{28,24},{20,28},{12,20},{4,12},{0,4},{9,1},{1... | collective-permute-start | bytes 2162696 | tf_op jit(solution)/shard_map/ppermute | solution.py:75
  159.3 43.0 %collective-permute-start.20 = (bf16[256,1408]{1,0:T(8,128)(2,1)S(1)}, bf16[256,1408]{1,0:T(8,128)(2,1)}, u32[]{:S(2)}, u32[]{:S(2)}) collective-permute-start(bf16[256,1408]{1,0:T(8,128)(2,1)S(1)} %collective-permute-done.14.refs_10_), channel_id=1, source_target_pairs={{0,8},{8,16},{16,24},{24,28},{28,20},{20,12},{12,4},{4,0},{1,9},{9... | collective-permute-start | bytes 2162696 | tf_op jit(solution)/shard_map/ppermute | solution.py:75
  160.9 41.4 %collective-permute-start.21 = (bf16[256,1408]{1,0:T(8,128)(2,1)S(1)}, bf16[256,1408]{1,0:T(8,128)(2,1)}, u32[]{:S(2)}, u32[]{:S(2)}) collective-permute-start(bf16[256,1408]{1,0:T(8,128)(2,1)S(1)} %collective-permute-done.15.refs_11_), channel_id=1, source_target_pairs={{8,0},{16,8},{24,16},{28,24},{20,28},{12,20},{4,12},{0,4},{9,1},{1... | collective-permute-start | bytes 2162696 | tf_op jit(solution)/shard_map/ppermute | solution.py:75
  183.6 34.2 %collective-permute-start.22 = (bf16[256,1408]{1,0:T(8,128)(2,1)S(1)}, bf16[256,1408]{1,0:T(8,128)(2,1)}, u32[]{:S(2)}, u32[]{:S(2)}) collective-permute-start(bf16[256,1408]{1,0:T(8,128)(2,1)S(1)} %collective-permute-done.18.refs_4_), channel_id=1, source_target_pairs={{0,8},{8,16},{16,24},{24,28},{28,20},{20,12},{12,4},{4,0},{1,9},{9... | collective-permute-start | bytes 2162696 | tf_op jit(solution)/shard_map/ppermute | solution.py:75
  184.8 33.0 %collective-permute-start.23 = (bf16[256,1408]{1,0:T(8,128)(2,1)}, bf16[256,1408]{1,0:T(8,128)(2,1)}, u32[]{:S(2)}, u32[]{:S(2)}) collective-permute-start(bf16[256,1408]{1,0:T(8,128)(2,1)} %collective-permute-done.19.refs_5_), channel_id=1, source_target_pairs={{8,0},{16,8},{24,16},{28,24},{20,28},{12,20},{4,12},{0,4},{9,1},{1... | collective-permute-start | bytes 2162696 | tf_op jit(solution)/shard_map/ppermute | solution.py:75
  217.8 98.3 %all-gather.13.cloned.1.call-start = ((), (), s32[]{:S(2)}) async-start(), calls=%async_computation.7 | async-start | bytes 3932160 | tf_op jit(solution)/shard_map/all_gather | solution.py:566
  258.8 164.8 %reduce-scatter.7.cloned.1.call-start = ((), (), s32[]{:S(2)}) async-start(), calls=%async_computation.8 | async-start | bytes 3932160 | tf_op jit(solution)/shard_map/reduce_scatter | solution.py:562
  388.8 82.8 %all-gather.15.cloned.1.call-start = ((), (), s32[]{:S(2)}) async-start(), calls=%async_computation.9 | async-start | bytes 3932160 | tf_op jit(solution)/shard_map/all_gather | solution.py:566
  428.1 115.0 %all-gather.19.cloned.1.call-start = ((), (), s32[]{:S(2)}) async-start(), calls=%async_computation.13 | async-start | bytes 1179648 | tf_op jit(solution)/shard_map/all_gather | solution.py:862
  467.9 36.2 %collective-permute-start.62 = (bf16[256,1408]{1,0:T(8,128)(2,1)}, bf16[256,1408]{1,0:T(8,128)(2,1)}, u32[]{:S(2)}, u32[]{:S(2)}) collective-permute-start(bf16[256,1408]{1,0:T(8,128)(2,1)} %fusion.7), channel_id=1, source_target_pairs={{0,8},{8,16},{16,24},{24,28},{28,20},{20,12},{12,4},{4,0},{1,9},{9... | collective-permute-start | bytes 2162696 | tf_op jit(solution)/shard_map/ppermute | solution.py:75
  471.0 36.5 %collective-permute-start.63 = (bf16[256,1408]{1,0:T(8,128)(2,1)}, bf16[256,1408]{1,0:T(8,128)(2,1)}, u32[]{:S(2)}, u32[]{:S(2)}) collective-permute-start(bf16[256,1408]{1,0:T(8,128)(2,1)} %fusion.8), channel_id=1, source_target_pairs={{8,0},{16,8},{24,16},{28,24},{20,28},{12,20},{4,12},{0,4},{9,1},{1... | collective-permute-start | bytes 2162696 | tf_op jit(solution)/shard_map/ppermute | solution.py:75
  496.5 183.0 %reduce-scatter.9.cloned.1.call-start = ((), (), s32[]{:S(2)}) async-start(), calls=%async_computation.10 | async-start | bytes 3932160 | tf_op jit(solution)/shard_map/reduce_scatter | solution.py:562
  507.6 40.2 %collective-permute-start.66 = (bf16[256,1408]{1,0:T(8,128)(2,1)}, bf16[256,1408]{1,0:T(8,128)(2,1)}, u32[]{:S(2)}, u32[]{:S(2)}) collective-permute-start(bf16[256,1408]{1,0:T(8,128)(2,1)} %fusion.11), channel_id=1, source_target_pairs={{0,8},{8,16},{16,24},{24,28},{28,20},{20,12},{12,4},{4,0},{1,9},{9... | collective-permute-start | bytes 2162696 | tf_op jit(solution)/shard_map/ppermute | solution.py:75
  511.9 38.3 %collective-permute-start.67 = (bf16[256,1408]{1,0:T(8,128)(2,1)}, bf16[256,1408]{1,0:T(8,128)(2,1)}, u32[]{:S(2)}, u32[]{:S(2)}) collective-permute-start(bf16[256,1408]{1,0:T(8,128)(2,1)} %fusion.12), channel_id=1, source_target_pairs={{8,0},{16,8},{24,16},{28,24},{20,28},{12,20},{4,12},{0,4},{9,1},{1... | collective-permute-start | bytes 2162696 | tf_op jit(solution)/shard_map/ppermute | solution.py:75
  531.4 32.9 %collective-permute-start.69 = (bf16[256,1408]{1,0:T(8,128)(2,1)}, bf16[256,1408]{1,0:T(8,128)(2,1)}, u32[]{:S(2)}, u32[]{:S(2)}) collective-permute-start(bf16[256,1408]{1,0:T(8,128)(2,1)} %fusion.14), channel_id=1, source_target_pairs={{8,0},{16,8},{24,16},{28,24},{20,28},{12,20},{4,12},{0,4},{9,1},{1... | collective-permute-start | bytes 2162696 | tf_op jit(solution)/shard_map/ppermute | solution.py:75
  543.1 139.0 %reduce-scatter.11.cloned.1.call-start = ((), (), s32[]{:S(2)}) async-start(), calls=%async_computation.11 | async-start | bytes 3932160 | tf_op jit(solution)/shard_map/reduce_scatter | solution.py:562
  615.8 34.6 %collective-permute-start.76 = (bf16[256,1280]{1,0:T(8,128)(2,1)}, bf16[256,1280]{1,0:T(8,128)(2,1)}, u32[]{:S(2)}, u32[]{:S(2)}) collective-permute-start(bf16[256,1280]{1,0:T(8,128)(2,1)} %pad_maximum_fusion.11), channel_id=1, source_target_pairs={{0,8},{8,16},{16,24},{24,28},{28,20},{20,12},{12,4},{4,0},{1,9},{9... | collective-permute-start | bytes 1966088 | tf_op jit(solution)/shard_map/ppermute | solution.py:75
  635.6 42.1 %collective-permute-start.74 = (bf16[256,1280]{1,0:T(8,128)(2,1)S(1)}, bf16[256,1280]{1,0:T(8,128)(2,1)S(1)}, u32[]{:S(2)}, u32[]{:S(2)}) collective-permute-start(bf16[256,1280]{1,0:T(8,128)(2,1)S(1)} %pad_maximum_fusion.8), channel_id=1, source_target_pairs={{0,8},{8,16},{16,24},{24,28},{28,20},{20,12},{12,4},{4,0},{1,9},{9... | collective-permute-start | bytes 1966088 | tf_op jit(solution)/shard_map/ppermute | solution.py:75
  640.3 35.5 %collective-permute-start.75 = (bf16[256,1280]{1,0:T(8,128)(2,1)S(1)}, bf16[256,1280]{1,0:T(8,128)(2,1)S(1)}, u32[]{:S(2)}, u32[]{:S(2)}) collective-permute-start(bf16[256,1280]{1,0:T(8,128)(2,1)S(1)} %pad_maximum_fusion.10), channel_id=1, source_target_pairs={{8,0},{16,8},{24,16},{28,24},{20,28},{12,20},{4,12},{0,4},{9,1},{1... | collective-permute-start | bytes 1966088 | tf_op jit(solution)/shard_map/ppermute | solution.py:75
  (161 other events, 3013.8 us)
Sparse Core Ops, SparseCore 0:
  11.2 31.2 all-gather.8
  44.7 28.5 all-gather.10
  134.3 47.7 all-gather.16
  217.9 36.9 reduce-scatter.4
  258.9 28.5 all-gather.12
  388.9 34.6 reduce-scatter.6
  428.2 28.5 all-gather.14
  496.6 46.0 all-gather.18
  545.2 39.2 reduce-scatter.8
  621.8 36.3 reduce-scatter.10

commit v3 on v2

--- a/solution.py
+++ b/solution.py
@@ -114,15 +114,22 @@
     for _ in range(count):
         for lane in lanes:
             lane.turn(*after)
+        groups = lanes[0].ring.groups
+        if len(lanes) == 2 and len(groups[-1]) == len(groups[-2]) == 1:
+            groups[-2:] = [groups[-2] + groups[-1]]
 
 
 def then(lanes, turn, *values):
+    if turn < 1:
+        return values if len(values) > 1 else values[0]
     waits = [v for lane in lanes for v in lane.got[turn - 1]]
     out = lax.optimization_barrier((*values, *waits))[: len(values)]
     return out if len(values) > 1 else out[0]
 
 
 def behind(lanes, turn, *values):
+    if turn < 1:
+        return values if len(values) > 1 else values[0]
     waits = [v for lane in lanes for v in lane.gave[turn - 1]]
     out = lax.optimization_barrier((*values, *waits))[: len(values)]
     return out if len(values) > 1 else out[0]
@@ -666,8 +673,7 @@
         mixer_full = [lane.end() for lane in mixer]
         pair_stack, other_stack = [[(full, 0, pair)] for full in mixer_full]
         output_stack = [(full, pair, pair + part) for full in mixer_full]
-        turns(glu, half)
-        turns(down, half - 1)
+        turns(glu, 1, *[lane.got[-1][0] for lane in mixer])
 
         state_shape = (blocks * wide, HD)
         factor = factors[0]
@@ -734,8 +740,7 @@
             ],
             flops=2 * rows * D * 2 * wide,
         )
-        inner = then(glu[1:], 1, inner)
-        message = then(glu[:1], 2, message)
+        turns(glu, 1, inner)
         mixer_out, squares, used = by_block(
             functools.partial(states_kernel, heads),
             [
@@ -752,7 +757,8 @@
             [pltpu.VMEM((wide, HD), f32)],
             flops=2 * rows * D * wide // 4,
         )
-        squares = then(glu[1:], 2, squares)
+        turns(glu[:1], half - 3)
+        turns(glu[1:], half - 3, squares)
         squares = lax.psum(jnp.sum(squares, axis=1), "tp")
         mixer_scale = lax.rsqrt(squares / D + NORM_EPS)[:, None]
         joined, branch_here = by_block(
@@ -762,11 +768,14 @@
             [((rows, wide), bf16, True), ((rows, D), bf16, True)],
             flops=2 * rows * D * wide,
         )
+        turns(glu, 1, branch_here)
+        turns(down, 1)
         branch = scatter_rows(then(glu[:1], 3, branch_here))
-        middle = inputs_here.astype(f32) + then(glu, half, branch).astype(f32)
+        middle = inputs_here.astype(f32) + then(glu, half - 1, branch).astype(f32)
         normed_two, scale_two = normalize(middle)
         rows_two_here = normed_two.astype(bf16)
         rows_two = gather_rows(rows_two_here)
+        turns(down, half - 3, rows_two_here)
         rows_two = then(down, 1, rows_two)
 
         glu_stack = [(lane.end(), 0, hidden) for lane in glu]
@@ -778,7 +787,7 @@
             flops=2 * rows * D * 2 * hidden,
         )
 
-        product = then(down, half - 1, product)
+        turns(down, 1, product)
         turns(down, 1)
         down_parts = [lane.end() for lane in down]
         down_stack = [(full, 0, full[0].shape[1]) for full in down_parts]
@@ -801,7 +810,7 @@
             [((rows, 2 * hidden), bf16, True)],
             flops=2 * rows * D * hidden,
         )
-        both_grads = then(down_total, 1, both_grads)
+        both_grads = then(down_total, 0, both_grads)
         turns(down_total, 1)
         glu_total = [
             Line(
@@ -830,7 +839,7 @@
         )
         branch_grad = gather_rows(middle_grad.astype(bf16))
         turns(glu_total, 1)
-        branch_grad = then(glu_total[:1], 2, branch_grad)
+        branch_grad = then(glu_total[:1], 0, branch_grad)
 
         gate_grad, inward, dots = by_block(
             joined_back_kernel,
@@ -897,7 +906,7 @@
                 Rows(values),
                 Rows(scaled_k),
                 Rows(kept),
-                then(glu_total[:1], half, all_back),
+                then(glu_total[1:], 1, all_back),
                 Rows(key_pre),
                 Rows(mask_col),
                 Rows(tail),
@@ -950,7 +959,7 @@
             one_grad,
         )
 
-        turns(mixer_total, 1, block_out, input_grad)
+        turns(mixer_total, 1)
         down_sum = jnp.concatenate([lane.end()[0] for lane in down_total], axis=1)
         glu_sum = jnp.stack([lane.end()[0] for lane in glu_total])
         (pair_sum, first_sum), (other_sum, second_sum) = [lane.end() for lane in mixer_total]
@@ -966,7 +975,7 @@
             output_weight, output_first, output_second, output_sum
         )
         glu_new, glu_first_new, glu_second_new = adamw_step(
-            glu_weight, glu_first, glu_second, then(mixer_total, 2, glu_sum)
+            glu_weight, glu_first, glu_second, then(mixer_total, 1, glu_sum)
         )
         down_new, down_first_new, down_second_new = adamw_across(
             down_weight, down_first, down_second, then(mixer_total, 1, down_sum)

time: 746 us -> 737 us (0.988)
  waiting for transfers between devices: 313 us -> 304 us
    ppermute x84, waiting for transfers between devices: 306 us -> 298 us  [send(): return lax.ppermute(value, 'seq', self.perms[way])]
  transfers between devices with their start and end apart: 94 -> 94, of which waited for: 57 -> 58; matrix products, arithmetic and copies ran while one was open for 18% -> 19% of each run, Pallas kernels for 17% -> 18%
where the time goes in v3:
time: 737 us; the launch traced here: 726 us
  waiting for transfers between devices  304 us (41%)
  Pallas kernels  152 us (21%)
  matrix products  103 us (14%)
  starting transfers between devices  88.4 us (12%)
  other arithmetic  38.5 us (5%)
  between operations  16.2 us (2%)
  local copies, waits for them, and re-layouts  12.5 us (2%)
  blocking collectives  12.2 us (2%)
    ppermute x84, waiting for transfers between devices, send(): return lax.ppermute(value, 'seq', self.perms[way])  298 us
    pallas_call x13, Pallas kernels, by_block(): pl.pallas_call(kernel, grid=(count,), in_specs=in_specs, out_specs=[spec(...  129 us
    dot_general x64, matrix products, mm(): return jnp.einsum(spec, a, b, preferred_element_type=f32)  102 us
    ppermute x84, starting transfers between devices, send(): return lax.ppermute(value, 'seq', self.perms[way])  87.8 us
  transfers between devices with their start and end apart: 94, of which 58 were waited for; matrix products, arithmetic and copies ran while one was open for 19% of the time, Pallas kernels for 18%

profile of v3, /device:TPU:0, one launch (start us, length us, event | category | flops | bytes accessed | tf_op | source)
XLA Modules:
  0.0 726.4 jit_solution(6331484071662584833)
XLA Ops:
  18.0 13.0 %collective-permute-done.refs_6_.refs_4_.refs_5_.refs_3_ = bf16[256,1280]{1,0:T(8,128)(2,1)S(1)} collective-permute-done((bf16[256,1280]{1,0:T(8,128)(2,1)S(1)}, bf16[256,1280]{1,0:T(8,128)(2,1)S(1)}, u32[]{:S(2)}, u32[]{:S(2)}) %collective-permute-start) | collective-permute-done | bytes 655392 | tf_op jit(solution)/shard_map/ppermute | solution.py:75
  35.2 9.9 %collective-permute-done.3.refs_6_.refs_12_.refs_13_.refs_11_ = bf16[256,1280]{1,0:T(8,128)(2,1)} collective-permute-done((bf16[256,1280]{1,0:T(8,128)(2,1)S(1)}, bf16[256,1280]{1,0:T(8,128)(2,1)}, u32[]{:S(2)}, u32[]{:S(2)}) %collective-permute-start.3) | collective-permute-done | bytes 655392 | tf_op jit(solution)/shard_map/ppermute | solution.py:75
  50.6 8.6 %collective-permute-done.2.refs_8_.refs_6_.refs_7_.refs_5_ = bf16[256,1280]{1,0:T(8,128)(2,1)} collective-permute-done((bf16[256,1280]{1,0:T(8,128)(2,1)S(1)}, bf16[256,1280]{1,0:T(8,128)(2,1)}, u32[]{:S(2)}, u32[]{:S(2)}) %collective-permute-start.2) | collective-permute-done | bytes 655392 | tf_op jit(solution)/shard_map/ppermute | solution.py:75
  63.4 9.8 %collective-permute-done.7.refs_8_.refs_14_.refs_15_.refs_13_ = bf16[256,1280]{1,0:T(8,128)(2,1)} collective-permute-done((bf16[256,1280]{1,0:T(8,128)(2,1)}, bf16[256,1280]{1,0:T(8,128)(2,1)}, u32[]{:S(2)}, u32[]{:S(2)}) %collective-permute-start.7) | collective-permute-done | bytes 655392 | tf_op jit(solution)/shard_map/ppermute | solution.py:75
  91.1 11.0 %collective-permute-done.11.refs_11_.refs_17_.refs_18_.refs_16_ = bf16[256,1280]{1,0:T(8,128)(2,1)} collective-permute-done((bf16[256,1280]{1,0:T(8,128)(2,1)}, bf16[256,1280]{1,0:T(8,128)(2,1)}, u32[]{:S(2)}, u32[]{:S(2)}) %collective-permute-start.11) | collective-permute-done | bytes 655392 | tf_op jit(solution)/shard_map/ppermute | solution.py:75
  103.5 10.9 %collective-permute-done.10.refs_12_.refs_10_.refs_11_.refs_9_ = bf16[256,1280]{1,0:T(8,128)(2,1)S(1)} collective-permute-done((bf16[256,1280]{1,0:T(8,128)(2,1)}, bf16[256,1280]{1,0:T(8,128)(2,1)S(1)}, u32[]{:S(2)}, u32[]{:S(2)}) %collective-permute-start.10) | collective-permute-done | bytes 655392 | tf_op jit(solution)/shard_map/ppermute | solution.py:75
  120.3 9.4 %shard_map.264 = (f32[768,512]{1,0:T(8,128)}, bf16[768,512]{1,0:T(8,128)(2,1)}, bf16[768,512]{1,0:T(8,128)(2,1)}, bf16[768,512]{1,0:T(8,128)(2,1)}, f32[1536,128]{1,0:T(8,128)}, /*index=5*/bf16[528,128]{1,0:T(8,128)(2,1)}) custom-call(bf16[768,2048]{1,0:T(8,128)(2,1)} %all-gather.9.cloned.1.call-done.refs_0_, f32[768,1]{1,0:T(8,128)} %bitcast.82, ...), custom_call_target="tpu_custom_call" | custom-call | tf_op jit(solution)/shard_map/pallas_call | solution.py:281
  137.8 10.1 %shard_map.265 = (f32[768,512]{1,0:T(8,128)}, f32[768,512]{1,0:T(8,128)}, bf16[768,512]{1,0:T(8,128)(2,1)}, bf16[768,512]{1,0:T(8,128)(2,1)}, bf16[768,1024]{1,0:T(8,128)(2,1)}, /*index=5*/f32[768,512]{1,0:T(8,128)}) custom-call(bf16[768,2048]{1,0:T(8,128)(2,1)} %all-gather.9.cloned.1.call-done.refs_0_, bf16[768,512]{1,0:T(8,128)(2,1)} %get-tuple-element.168.refs_1_, ...), custom_call_target="tpu_custom_call" | custom-call | tf_op jit(solution)/shard_map/pallas_call | solution.py:281
  150.2 8.1 %collective-permute-done.17.refs_10_ = bf16[256,1408]{1,0:T(8,128)(2,1)S(1)} collective-permute-done((bf16[256,1408]{1,0:T(8,128)(2,1)S(1)}, bf16[256,1408]{1,0:T(8,128)(2,1)S(1)}, u32[]{:S(2)}, u32[]{:S(2)}) %collective-permute-start.17) | collective-permute-done | bytes 720928 | tf_op jit(solution)/shard_map/ppermute | solution.py:75
  160.9 19.3 %collective-permute-done.16.refs_4_ = bf16[256,1408]{1,0:T(8,128)(2,1)} collective-permute-done((bf16[256,1408]{1,0:T(8,128)(2,1)S(1)}, bf16[256,1408]{1,0:T(8,128)(2,1)}, u32[]{:S(2)}, u32[]{:S(2)}) %collective-permute-start.16) | collective-permute-done | bytes 720928 | tf_op jit(solution)/shard_map/ppermute | solution.py:75
  209.5 15.5 %collective-permute-done.22.refs_12_ = bf16[256,1408]{1,0:T(8,128)(2,1)S(1)} collective-permute-done((bf16[256,1408]{1,0:T(8,128)(2,1)S(1)}, bf16[256,1408]{1,0:T(8,128)(2,1)S(1)}, u32[]{:S(2)}, u32[]{:S(2)}) %collective-permute-start.22) | collective-permute-done | bytes 720928 | tf_op jit(solution)/shard_map/ppermute | solution.py:75
  228.9 14.7 %collective-permute-done.24.refs_14_ = bf16[256,1408]{1,0:T(8,128)(2,1)S(1)} collective-permute-done((bf16[256,1408]{1,0:T(8,128)(2,1)S(1)}, bf16[256,1408]{1,0:T(8,128)(2,1)S(1)}, u32[]{:S(2)}, u32[]{:S(2)}) %collective-permute-start.24) | collective-permute-done | bytes 720928 | tf_op jit(solution)/shard_map/ppermute | solution.py:75
  253.7 12.3 %collective-permute-done.28.refs_8_ = bf16[256,1408]{1,0:T(8,128)(2,1)} collective-permute-done((bf16[256,1408]{1,0:T(8,128)(2,1)S(1)}, bf16[256,1408]{1,0:T(8,128)(2,1)}, u32[]{:S(2)}, u32[]{:S(2)}) %collective-permute-start.28) | collective-permute-done | bytes 720928 | tf_op jit(solution)/shard_map/ppermute | solution.py:75
  272.5 10.9 %collective-permute-done.26.refs_4_.refs_2_ = bf16[256,640]{1,0:T(8,128)(2,1)S(1)} collective-permute-done((bf16[256,640]{1,0:T(8,128)(2,1)S(1)}, bf16[256,640]{1,0:T(8,128)(2,1)S(1)}, u32[]{:S(2)}, u32[]{:S(2)}) %collective-permute-start.26) | collective-permute-done | bytes 327712 | tf_op jit(solution)/shard_map/ppermute | solution.py:75
  289.7 16.6 %shard_map.268 = (f32[768,1408]{1,0:T(8,128)}, f32[768,1408]{1,0:T(8,128)}, bf16[768,1408]{1,0:T(8,128)(2,1)}) custom-call(bf16[768,2048]{1,0:T(8,128)(2,1)} %all-gather.13.cloned.1.call-done.refs_0_, bf16[256,1408]{1,0:T(8,128)(2,1)} %copy-done.17, bf16[256,1408]{1,0:T(8,128)(2,1)} %copy-done.28, bf16[256,1408]{1,0:T(8,128)(2,1)} %collective-permute-done.15.refs_3_, ...), custom_call_target="tpu_custom_call" | custom-call | tf_op jit(solution)/shard_map/pallas_call | solution.py:281
  313.2 8.6 %collective-permute-done.34.refs_8_.refs_6_ = bf16[256,640]{1,0:T(8,128)(2,1)S(1)} collective-permute-done((bf16[256,640]{1,0:T(8,128)(2,1)}, bf16[256,640]{1,0:T(8,128)(2,1)S(1)}, u32[]{:S(2)}, u32[]{:S(2)}) %collective-permute-start.34) | collective-permute-done | bytes 327712 | tf_op jit(solution)/shard_map/ppermute | solution.py:75
  343.5 13.4 %shard_map.269.refs_0_ = bf16[768,2816]{1,0:T(8,128)(2,1)} custom-call(bf16[768,2048]{1,0:T(8,128)(2,1)} %all-gather.11.cloned.1.call-done.refs_0_, f32[768,1408]{1,0:T(8,128)} %get-tuple-element.199.refs_1_, f32[768,1408]{1,0:T(8,128)} %get-tuple-element.200.refs_2_, bf16[256,640]{1,0:T(8,128)(2,1)} %copy-done.27, bf16[256,640]{1,0:T(8,128)(2,1)} %copy-done.57, ...), custom_call_target="tpu_custom_call" | custom-call | tf_op jit(solution)/shard_map/pallas_call | solution.py:281
  368.6 16.4 %shard_map.270 = bf16[768,2048]{1,0:T(8,128)(2,1)} custom-call(bf16[768,2816]{1,0:T(8,128)(2,1)} %shard_map.269.refs_0_, bf16[256,1408]{1,0:T(8,128)(2,1)} %copy-done.17, bf16[256,1408]{1,0:T(8,128)(2,1)} %copy-done.28, bf16[256,1408]{1,0:T(8,128)(2,1)} %collective-permute-done.15.refs_3_, bf16[256,1408]{1,0:T(8,128)(2,1)} %collective-permute-done.16.refs_4_, ...), custom_call_target="tpu_custom_call" | custom-call | tf_op jit(solution)/shard_map/pallas_call | solution.py:281
  453.8 8.4 %collective-permute-done.60 = bf16[256,1408]{1,0:T(8,128)(2,1)S(1)} collective-permute-done((bf16[256,1408]{1,0:T(8,128)(2,1)S(1)}, bf16[256,1408]{1,0:T(8,128)(2,1)S(1)}, u32[]{:S(2)}, u32[]{:S(2)}) %collective-permute-start.60) | collective-permute-done | bytes 720928 | tf_op jit(solution)/shard_map/ppermute | solution.py:75
  508.3 9.5 %collective-permute-done.64 = bf16[256,1408]{1,0:T(8,128)(2,1)S(1)} collective-permute-done((bf16[256,1408]{1,0:T(8,128)(2,1)S(1)}, bf16[256,1408]{1,0:T(8,128)(2,1)S(1)}, u32[]{:S(2)}, u32[]{:S(2)}) %collective-permute-start.64) | collective-permute-done | bytes 720928 | tf_op jit(solution)/shard_map/ppermute | solution.py:75
  528.6 10.5 %shard_map.273 = bf16[768,2048]{1,0:T(8,128)(2,1)} custom-call(bf16[768,1408]{1,0:T(8,128)(2,1)} %get-tuple-element.237.refs_0_, bf16[256,640]{1,0:T(8,128)(2,1)} %copy-done.27, bf16[256,640]{1,0:T(8,128)(2,1)} %copy-done.57, bf16[256,640]{1,0:T(8,128)(2,1)} %collective-permute-done.27.refs_5_.refs_3_, ...), custom_call_target="tpu_custom_call" | custom-call | tf_op jit(solution)/shard_map/pallas_call | solution.py:281
  589.8 13.0 %shard_map.277 = bf16[768,2048]{1,0:T(8,128)(2,1)} custom-call(bf16[768,1024]{1,0:T(8,128)(2,1)} %get-tuple-element.273.refs_0_, bf16[768,1024]{1,0:T(8,128)(2,1)} %get-tuple-element.271.refs_1_, bf16[256,1280]{1,0:T(8,128)(2,1)} %copy-done.4, bf16[256,1280]{1,0:T(8,128)(2,1)} %copy-done.10, bf16[256,1280]{1,0:T(8,128)(2,1)} %copy-done.11, ...), custom_call_target="tpu_custom_call" | custom-call | tf_op jit(solution)/shard_map/pallas_call | solution.py:281
  646.9 12.6 %collective-permute-done.79 = bf16[256,1280]{1,0:T(8,128)(2,1)S(1)} collective-permute-done((bf16[256,1280]{1,0:T(8,128)(2,1)S(1)}, bf16[256,1280]{1,0:T(8,128)(2,1)S(1)}, u32[]{:S(2)}, u32[]{:S(2)}) %collective-permute-start.79) | collective-permute-done | bytes 655392 | tf_op jit(solution)/shard_map/ppermute | solution.py:75
  681.0 9.1 %shard_map.280 = (f32[1408,256]{1,0:T(8,128)}, f32[1408,256]{1,0:T(8,128)}, f32[1408,256]{1,0:T(8,128)}) custom-call(f32[1408,256]{1,0:T(8,128)} %w.3, f32[1408,256]{1,0:T(8,128)} %m.3, f32[1408,256]{1,0:T(8,128)} %v.3, f32[256,1408]{1,0:T(8,128)} %pad_maximum_fusion.2.g), custom_call_target="tpu_custom_call" | custom-call | tf_op jit(solution)/shard_map/pallas_call | solution.py:595
  (510 shorter events, 428.5 us)
Async XLA Ops:
  7.2 113.1 %all-gather.9.cloned.1.call-start = ((), (), s32[]{:S(2)}) async-start(), calls=%async_computation.4 | async-start | bytes 3932160 | tf_op jit(solution)/shard_map/all_gather | solution.py:573
  11.2 123.5 %all-gather.11.cloned.1.call-start = ((), (), s32[]{:S(2)}) async-start(), calls=%async_computation.5 | async-start | bytes 3932160 | tf_op jit(solution)/shard_map/all_gather | solution.py:573
  11.9 173.4 %all-gather.17.cloned.1.call-start = ((), (), s32[]{:S(2)}) async-start(), calls=%async_computation.12 | async-start | bytes 1216512 | tf_op jit(solution)/shard_map/all_gather | solution.py:708
  15.6 29.6 %collective-permute-start.3 = (bf16[256,1280]{1,0:T(8,128)(2,1)S(1)}, bf16[256,1280]{1,0:T(8,128)(2,1)}, u32[]{:S(2)}, u32[]{:S(2)}) collective-permute-start(bf16[256,1280]{1,0:T(8,128)(2,1)S(1)} %pad_maximum_fusion.4.refs_5_.refs_11_.refs_12_.refs_10_), channel_id=1, source_target_pairs={{0,8},{8,16},{16,24},{24,28},{28,20},{20,12},{12,4},{4,0},{1,9},{9... | collective-permute-start | bytes 1966088 | tf_op jit(solution)/shard_map/ppermute | solution.py:75
  17.7 29.7 %collective-permute-start.4 = (bf16[256,1280]{1,0:T(8,128)(2,1)S(1)}, bf16[256,1280]{1,0:T(8,128)(2,1)}, u32[]{:S(2)}, u32[]{:S(2)}) collective-permute-start(bf16[256,1280]{1,0:T(8,128)(2,1)S(1)} %pad_maximum_fusion.4.refs_5_.refs_11_.refs_12_.refs_10_), channel_id=1, source_target_pairs={{8,0},{16,8},{24,16},{28,24},{20,28},{12,20},{4,12},{0,4},{9,1},{1... | collective-permute-start | bytes 1966088 | tf_op jit(solution)/shard_map/ppermute | solution.py:75
  134.8 109.8 %reduce-scatter.5.cloned.1.call-start = ((), (), s32[]{:S(2)}) async-start(), calls=%async_computation.6 | async-start | bytes 3932160 | tf_op jit(solution)/shard_map/reduce_scatter | solution.py:569
  147.9 32.2 %collective-permute-start.16 = (bf16[256,1408]{1,0:T(8,128)(2,1)S(1)}, bf16[256,1408]{1,0:T(8,128)(2,1)}, u32[]{:S(2)}, u32[]{:S(2)}) collective-permute-start(bf16[256,1408]{1,0:T(8,128)(2,1)S(1)} %collective-permute-done.14.refs_2_), channel_id=1, source_target_pairs={{0,8},{8,16},{16,24},{24,28},{28,20},{20,12},{12,4},{4,0},{1,9},{9... | collective-permute-start | bytes 2162696 | tf_op jit(solution)/shard_map/ppermute | solution.py:75
  149.5 33.8 %collective-permute-start.19 = (bf16[256,1408]{1,0:T(8,128)(2,1)}, bf16[256,1408]{1,0:T(8,128)(2,1)}, u32[]{:S(2)}, u32[]{:S(2)}) collective-permute-start(bf16[256,1408]{1,0:T(8,128)(2,1)} %collective-permute-done.15.refs_3_), channel_id=1, source_target_pairs={{8,0},{16,8},{24,16},{28,24},{20,28},{12,20},{4,12},{0,4},{9,1},{1... | collective-permute-start | bytes 2162696 | tf_op jit(solution)/shard_map/ppermute | solution.py:75
  207.4 82.3 %all-gather.13.cloned.1.call-start = ((), (), s32[]{:S(2)}) async-start(), calls=%async_computation.7 | async-start | bytes 3932160 | tf_op jit(solution)/shard_map/all_gather | solution.py:573
  249.3 170.1 %reduce-scatter.7.cloned.1.call-start = ((), (), s32[]{:S(2)}) async-start(), calls=%async_computation.8 | async-start | bytes 3932160 | tf_op jit(solution)/shard_map/reduce_scatter | solution.py:569
  385.0 82.6 %all-gather.15.cloned.1.call-start = ((), (), s32[]{:S(2)}) async-start(), calls=%async_computation.9 | async-start | bytes 3932160 | tf_op jit(solution)/shard_map/all_gather | solution.py:573
  423.9 115.2 %all-gather.19.cloned.1.call-start = ((), (), s32[]{:S(2)}) async-start(), calls=%async_computation.13 | async-start | bytes 1179648 | tf_op jit(solution)/shard_map/all_gather | solution.py:871
  449.0 28.6 %collective-permute-start.58 = (bf16[256,1408]{1,0:T(8,128)(2,1)S(1)}, bf16[256,1408]{1,0:T(8,128)(2,1)S(1)}, u32[]{:S(2)}, u32[]{:S(2)}) collective-permute-start(bf16[256,1408]{1,0:T(8,128)(2,1)S(1)} %convolution_convert_fusion.1), channel_id=1, source_target_pairs={{0,8},{8,16},{16,24},{24,28},{28,20},{20,12},{12,4},{4,0},{1,9},{9... | collective-permute-start | bytes 2162696 | tf_op jit(solution)/shard_map/ppermute | solution.py:75
  450.5 28.6 %collective-permute-start.59 = (bf16[256,1408]{1,0:T(8,128)(2,1)}, bf16[256,1408]{1,0:T(8,128)(2,1)S(1)}, u32[]{:S(2)}, u32[]{:S(2)}) collective-permute-start(bf16[256,1408]{1,0:T(8,128)(2,1)} %fusion.5), channel_id=1, source_target_pairs={{8,0},{16,8},{24,16},{28,24},{20,28},{12,20},{4,12},{0,4},{9,1},{1... | collective-permute-start | bytes 2162696 | tf_op jit(solution)/shard_map/ppermute | solution.py:75
  463.9 36.2 %collective-permute-start.62 = (bf16[256,1408]{1,0:T(8,128)(2,1)}, bf16[256,1408]{1,0:T(8,128)(2,1)}, u32[]{:S(2)}, u32[]{:S(2)}) collective-permute-start(bf16[256,1408]{1,0:T(8,128)(2,1)} %fusion.6), channel_id=1, source_target_pairs={{0,8},{8,16},{16,24},{24,28},{28,20},{20,12},{12,4},{4,0},{1,9},{9... | collective-permute-start | bytes 2162696 | tf_op jit(solution)/shard_map/ppermute | solution.py:75
  467.1 36.5 %collective-permute-start.63 = (bf16[256,1408]{1,0:T(8,128)(2,1)}, bf16[256,1408]{1,0:T(8,128)(2,1)}, u32[]{:S(2)}, u32[]{:S(2)}) collective-permute-start(bf16[256,1408]{1,0:T(8,128)(2,1)} %fusion.8), channel_id=1, source_target_pairs={{8,0},{16,8},{24,16},{28,24},{20,28},{12,20},{4,12},{0,4},{9,1},{1... | collective-permute-start | bytes 2162696 | tf_op jit(solution)/shard_map/ppermute | solution.py:75
  492.5 220.2 %reduce-scatter.9.cloned.1.call-start = ((), (), s32[]{:S(2)}) async-start(), calls=%async_computation.10 | async-start | bytes 3932160 | tf_op jit(solution)/shard_map/reduce_scatter | solution.py:569
  503.5 40.2 %collective-permute-start.66 = (bf16[256,1408]{1,0:T(8,128)(2,1)}, bf16[256,1408]{1,0:T(8,128)(2,1)}, u32[]{:S(2)}, u32[]{:S(2)}) collective-permute-start(bf16[256,1408]{1,0:T(8,128)(2,1)} %fusion.11), channel_id=1, source_target_pairs={{0,8},{8,16},{16,24},{24,28},{28,20},{20,12},{12,4},{4,0},{1,9},{9... | collective-permute-start | bytes 2162696 | tf_op jit(solution)/shard_map/ppermute | solution.py:75
  507.8 38.3 %collective-permute-start.67 = (bf16[256,1408]{1,0:T(8,128)(2,1)}, bf16[256,1408]{1,0:T(8,128)(2,1)}, u32[]{:S(2)}, u32[]{:S(2)}) collective-permute-start(bf16[256,1408]{1,0:T(8,128)(2,1)} %fusion.12), channel_id=1, source_target_pairs={{8,0},{16,8},{24,16},{28,24},{20,28},{12,20},{4,12},{0,4},{9,1},{1... | collective-permute-start | bytes 2162696 | tf_op jit(solution)/shard_map/ppermute | solution.py:75
  524.9 30.8 %collective-permute-start.68 = (bf16[256,1408]{1,0:T(8,128)(2,1)}, bf16[256,1408]{1,0:T(8,128)(2,1)}, u32[]{:S(2)}, u32[]{:S(2)}) collective-permute-start(bf16[256,1408]{1,0:T(8,128)(2,1)} %fusion.13), channel_id=1, source_target_pairs={{0,8},{8,16},{16,24},{24,28},{28,20},{20,12},{12,4},{4,0},{1,9},{9... | collective-permute-start | bytes 2162696 | tf_op jit(solution)/shard_map/ppermute | solution.py:75
  527.4 32.9 %collective-permute-start.69 = (bf16[256,1408]{1,0:T(8,128)(2,1)}, bf16[256,1408]{1,0:T(8,128)(2,1)}, u32[]{:S(2)}, u32[]{:S(2)}) collective-permute-start(bf16[256,1408]{1,0:T(8,128)(2,1)} %fusion.14), channel_id=1, source_target_pairs={{8,0},{16,8},{24,16},{28,24},{20,28},{12,20},{4,12},{0,4},{9,1},{1... | collective-permute-start | bytes 2162696 | tf_op jit(solution)/shard_map/ppermute | solution.py:75
  539.2 176.2 %reduce-scatter.11.cloned.1.call-start = ((), (), s32[]{:S(2)}) async-start(), calls=%async_computation.11 | async-start | bytes 3932160 | tf_op jit(solution)/shard_map/reduce_scatter | solution.py:569
  611.8 30.0 %collective-permute-start.76 = (bf16[256,1280]{1,0:T(8,128)(2,1)}, bf16[256,1280]{1,0:T(8,128)(2,1)}, u32[]{:S(2)}, u32[]{:S(2)}) collective-permute-start(bf16[256,1280]{1,0:T(8,128)(2,1)} %pad_maximum_fusion.11), channel_id=1, source_target_pairs={{0,8},{8,16},{16,24},{24,28},{28,20},{20,12},{12,4},{4,0},{1,9},{9... | collective-permute-start | bytes 1966088 | tf_op jit(solution)/shard_map/ppermute | solution.py:75
  630.7 30.5 %collective-permute-start.74 = (bf16[256,1280]{1,0:T(8,128)(2,1)S(1)}, bf16[256,1280]{1,0:T(8,128)(2,1)S(1)}, u32[]{:S(2)}, u32[]{:S(2)}) collective-permute-start(bf16[256,1280]{1,0:T(8,128)(2,1)S(1)} %pad_maximum_fusion.8), channel_id=1, source_target_pairs={{0,8},{8,16},{16,24},{24,28},{28,20},{20,12},{12,4},{4,0},{1,9},{9... | collective-permute-start | bytes 1966088 | tf_op jit(solution)/shard_map/ppermute | solution.py:75
  (156 other events, 2580.4 us)
Sparse Core Ops, SparseCore 0:
  11.3 31.2 all-gather.8
  44.7 28.6 all-gather.10
  134.9 44.6 all-gather.16
  207.5 36.3 reduce-scatter.4
  249.5 27.0 all-gather.12
  385.2 34.2 reduce-scatter.6
  424.1 28.5 all-gather.14
  492.6 46.0 all-gather.18
  541.2 39.2 reduce-scatter.8
  617.8 36.3 reduce-scatter.10
